TPU v7x, 128 devices: a whole 4x4x4 slice. The times are simulated.
128 devices in a mesh: seq: 64 (over y, x, z), head: 2 (over core).
Axes of the slice: x: 4, y: 4, z: 4, core: 2. Of those that a mesh axis runs over, the one named last changes fastest.
Arguments:
- queries: bfloat16 [32768, 2048], P('seq', 'head'), may hold values from -8 to 8
- keys: bfloat16 [32768, 2048], P('seq', 'head'), may hold values from -8 to 8
- values: bfloat16 [32768, 2048], P('seq', 'head'), may hold values from -6 to 6
- out_grad: bfloat16 [32768, 2048], P('seq', 'head'), may hold values from -6 to 6
- cluster_ids: int32 [16, 32768, 1], P('head', 'seq'), may hold values from 0 to 255; in each aligned block of 512 rows (0 to 511, 512 to 1023, ..., all dimensions but the last counted through in order) at most 4 rows name the same one
- cluster_slot: int32 [256], replicated, may hold values from 0 to 255, each once
- centroids: float32 [16, 256, 128], P('head', 'seq'), may hold values from -6 to 6
Outputs:
- layer_out: bfloat16 [32768, 2048], P('seq', 'head')
- grad_queries: bfloat16 [32768, 2048], P('seq', 'head')
- grad_keys: bfloat16 [32768, 2048], P('seq', 'head')
- grad_values: bfloat16 [32768, 2048], P('seq', 'head')
- new_centroids: float32 [16, 256, 128], P('head', 'seq')
Inputs may be any that keep to these rules, and one draw needn't show every extreme that they name: `cluster_ids`: for each head, among the tokens of one device no cluster is named more than 4 times, a bound that some block reaches. `cluster_slot`: each slot is taken by one cluster.
All inputs are finite; a program needn't handle non-finite values.
Results may differ from a plain program's by a relative error of at most 0.024.
The roundings to bfloat16 on the way count: a program that leaves them out, or rounds other values in their place, can miss the bound.
Values may be sent and summed in bfloat16 or wider, within the bound.
No kernel may reach another device: no remote copies, remote signals or barrier semaphores. Data moves between devices by JAX's collectives and lax.ppermute only.
A program may use at most 128 MiB of HBM per device.

v0:
```python
import functools
import math

import jax
import jax.numpy as jnp
from jax import lax
from jax.experimental import pallas as pl
from jax.experimental.pallas import tpu as pltpu
from jax.sharding import PartitionSpec as P

CAP = 4
DECAY_RATE = 0.9
MASKED = -1e30
ABSENT = 64.0
CHUNKS = 2
SHARED = 8
PACKED = 16
SPARE = 2
PEAK_LANE = 127
TURN_BY = 8
VMEM_BYTES = 63 * 1024 * 1024
LESS_VMEM_BYTES = 40 * 1024 * 1024

F32 = jnp.float32
BF16 = jnp.bfloat16
CONTRACT_LAST = (((1,), (1,)), ((), ()))
CONTRACT_FIRST = (((0,), (0,)), ((), ()))


def iota(shape, dim):
    return lax.broadcasted_iota(jnp.int32, shape, dim)


def dot(left, right):
    return jnp.dot(left, right, preferred_element_type=F32)


def pack_kernel(ids_ref, slot_ref, q_ref, k_ref, v_ref, g_ref, send_ref, flat_ref, earlier_ref):
    tok_rows = ids_ref.shape[2]
    cluster_count = slot_ref.shape[1]
    slot_rows = cluster_count * CAP

    @pl.when(pl.program_id(0) == 0)
    def _():
        earlier_ref[...] = (iota((tok_rows, tok_rows), 0) < iota((tok_rows, tok_rows), 1)).astype(
            F32
        ).astype(BF16)

    ids_row = ids_ref[0]
    member = iota((cluster_count, tok_rows), 0) == ids_row
    member_f = jnp.where(member, 1.0, 0.0)
    member_low = member_f.astype(BF16)
    slots_low = jnp.broadcast_to(slot_ref[...].astype(F32), (8, cluster_count)).astype(BF16)
    slot_row = dot(slots_low, member_low)[0:1]
    rank_row = jnp.sum(dot(member_low, earlier_ref[...]) * member_f, axis=0, keepdims=True)
    flat_row = (slot_row * CAP + rank_row).astype(jnp.int32)
    flat_ref[0] = flat_row
    place = jnp.where(iota((slot_rows, tok_rows), 0) == flat_row, 1.0, 0.0).astype(BF16)
    ones = jnp.ones((tok_rows, 128), BF16)
    head_size = q_ref.shape[1]
    taken = dot(place, ones)
    out_shape = send_ref.shape[:2] + (head_size,)

    def put(at, rows):
        send_ref[:, :, at * head_size : (at + 1) * head_size] = rows.astype(BF16).reshape(out_shape)

    put(0, dot(place, q_ref[...]))
    put(1, dot(place, k_ref[...]) + (1.0 - taken) * ABSENT)
    put(2, dot(place, v_ref[...]))
    put(3, dot(place, g_ref[...]))


def owner_kernel(recv_ref, cent_ref, back_ref, new_ref, turn_ref, causal_ref, rows_ref, grads_ref):
    source_count, block_rows, width = recv_ref.shape
    head_size = width // 4
    owned = block_rows // CAP
    slot_count = source_count * CAP
    group_rows = 16 * block_rows
    groups = source_count // 16
    part = 16 * CAP
    score_scale = 1.0 / math.sqrt(head_size)

    @pl.when(pl.program_id(0) == 0)
    def _():
        row_at = iota((group_rows, group_rows), 0)
        col_at = iota((group_rows, group_rows), 1)
        cluster_of = row_at // part
        source_of = (row_at % part) // CAP
        from_row = source_of * block_rows + cluster_of * CAP + row_at % CAP
        turn_ref[...] = jnp.where(from_row == col_at, 1.0, 0.0).astype(BF16)
        causal_ref[...] = jnp.where(
            iota((slot_count, slot_count), 1) <= iota((slot_count, slot_count), 0), 0.0, MASKED
        )

    turn = turn_ref[...]
    @pl.loop(0, groups)
    def _(group):
        arrived = recv_ref[pl.ds(group * 16, 16)].reshape(group_rows, width)
        turned = dot(turn, arrived).astype(BF16)
        at_row = pl.multiple_of(group * part, part)
        rows_ref[:, pl.ds(at_row, part), :] = turned.reshape(owned, part, width)

    first_lane = jnp.where(iota((8, head_size), 1) == 0, 1.0, 0.0).astype(BF16)
    @pl.loop(0, owned)
    def _(cluster):
        q = rows_ref[cluster, :, 0:head_size]
        k = rows_ref[cluster, :, head_size : 2 * head_size]
        v = rows_ref[cluster, :, 2 * head_size : 3 * head_size]
        g = rows_ref[cluster, :, 3 * head_size : 4 * head_size]
        marks = lax.dot_general(first_lane, k, CONTRACT_LAST, preferred_element_type=F32)
        present = marks < ABSENT / 2
        bias = jnp.where(present, 0.0, MASKED)[0:1]
        scores = lax.dot_general(q, k, CONTRACT_LAST, preferred_element_type=F32) * score_scale
        scores = scores + (causal_ref[...] + bias)
        weights = jnp.exp(scores - jnp.max(scores, axis=-1, keepdims=True))
        probs = weights / jnp.sum(weights, axis=-1, keepdims=True)
        probs_low = probs.astype(BF16)
        out = dot(probs_low, v).astype(BF16)
        grad_prob = lax.dot_general(g, v, CONTRACT_LAST, preferred_element_type=F32)
        delta = jnp.sum(g.astype(F32) * out.astype(F32), axis=-1, keepdims=True)
        grad_score = (probs * (grad_prob - delta) * score_scale).astype(BF16)
        grad_q = dot(grad_score, k)
        grad_k = lax.dot_general(grad_score, q, CONTRACT_FIRST, preferred_element_type=F32)
        grad_v = lax.dot_general(probs_low, g, CONTRACT_FIRST, preferred_element_type=F32)
        grads_ref[cluster, :, 0:head_size] = out
        grads_ref[cluster, :, head_size : 2 * head_size] = grad_q.astype(BF16)
        grads_ref[cluster, :, 2 * head_size : 3 * head_size] = grad_k.astype(BF16)
        grads_ref[cluster, :, 3 * head_size : 4 * head_size] = grad_v.astype(BF16)
        key_sums = dot(jnp.where(present, 1.0, 0.0).astype(BF16), k)[0:1]
        blend = DECAY_RATE * cent_ref[0, pl.ds(cluster, 1), :] + (1.0 - DECAY_RATE) * key_sums
        new_ref[0, pl.ds(cluster, 1), :] = blend / jnp.sqrt(
            jnp.mean(blend * blend, axis=-1, keepdims=True) + 1e-06
        )

    @pl.loop(0, groups)
    def _(group):
        at_row = pl.multiple_of(group * part, part)
        leaving = grads_ref[:, pl.ds(at_row, part), :].reshape(group_rows, width)
        turned = lax.dot_general(turn, leaving, CONTRACT_FIRST, preferred_element_type=F32)
        back_ref[pl.ds(group * 16, 16)] = turned.astype(BF16).reshape(16, block_rows, width)


def unpack_kernel(chunk, flat_ref, ret_ref, *refs):
    out_refs = refs[-4:]
    sources, block_rows, width = ret_ref.shape
    head_size = width // 4
    tok_rows, heads = flat_ref.shape
    slot_rows = sources * block_rows
    here = iota((tok_rows, heads), 1) == pl.program_id(0)
    flat_col = jnp.sum(jnp.where(here, flat_ref[...], 0), axis=1, keepdims=True)
    take = jnp.where(iota((tok_rows, slot_rows), 1) == flat_col, 1.0, 0.0).astype(BF16)
    rows = dot(take, ret_ref[...].reshape(slot_rows, width)).astype(BF16)
    for at, out_ref in enumerate(out_refs):
        out_ref[...] = rows[:, at * head_size : (at + 1) * head_size]


def find_rows(first_head, ids_ref, slot_ref, base_ref, over_ref, header_ref):
    heads, _, tok_rows = ids_ref.shape
    cluster_count = slot_ref.shape[1]
    owners, lanes = header_ref.shape
    earlier = jnp.where(
        iota((tok_rows, tok_rows), 0) < iota((tok_rows, tok_rows), 1), 1.0, 0.0
    ).astype(BF16)
    slots_low = jnp.broadcast_to(slot_ref[...].astype(F32), (8, cluster_count)).astype(BF16)
    members = [
        jnp.where(iota((cluster_count, tok_rows), 0) == ids_ref[head], 1.0, 0.0)
        for head in range(heads)
    ]
    member_low = jnp.concatenate(members, axis=0).astype(BF16)
    earlier_members = dot(member_low, earlier)
    owner_of, tag_of, here_of = [], [], []
    for head in range(heads):
        own = slice(head * cluster_count, (head + 1) * cluster_count)
        slot = dot(slots_low, member_low[own])[0:1].astype(jnp.int32)
        rank = jnp.sum(earlier_members[own] * members[head], axis=0, keepdims=True)
        owner = (slot // CAP + TURN_BY * (first_head + head)) % owners
        owner_of.append(owner)
        tag_of.append((head * CAP + slot % CAP) * CAP + rank.astype(jnp.int32))
        here_of.append(jnp.where(iota((owners, tok_rows), 0) == owner, 1.0, 0.0))
    before_all = dot(jnp.concatenate(here_of, axis=0).astype(BF16), earlier)
    filled = jnp.zeros((owners, 1), F32)
    header = jnp.zeros((owners, lanes), F32)
    for head in range(heads):
        here_f = here_of[head]
        before = before_all[head * owners : (head + 1) * owners]
        place = jnp.sum(before * here_f, axis=0, keepdims=True).astype(jnp.int32)
        late = jnp.sum((before + filled) * here_f, axis=0, keepdims=True)
        late = late.astype(jnp.int32) - SHARED
        filled = filled + jnp.maximum(jnp.sum(here_f, axis=1, keepdims=True) - SHARED, 0.0)
        fits = place < SHARED
        packs = (late < PACKED - SPARE) & (place >= SHARED)
        base_ref[head] = jnp.where(fits, owner_of[head] * SHARED + place, -1)
        over_ref[head] = jnp.where(packs, owner_of[head] * PACKED + late, -1)
        lane = jnp.where(fits, head * SHARED + place, jnp.where(packs, heads * SHARED + late, -1))
        named = (here_f * (tag_of[head] + 1).astype(F32)).astype(BF16)
        lane_at = jnp.where(iota((lanes, tok_rows), 0) == lane, 1.0, 0.0).astype(BF16)
        header = header + lax.dot_general(
            named, lane_at, CONTRACT_LAST, preferred_element_type=F32
        )
    peak = jnp.max(filled, axis=0, keepdims=True)
    header_ref[...] = jnp.where(iota((owners, lanes), 1) == PEAK_LANE, peak, header).astype(BF16)


def token_rows(columns_ref, step, at, head_size):
    lanes = slice(at * head_size, (at + 1) * head_size)
    parts = [columns_ref[step, which, :, lanes] for which in range(columns_ref.shape[1])]
    return jnp.concatenate(parts, axis=1)


def pack_rows_kernel(
    first_head,
    ids_ref,
    slot_ref,
    q_ref,
    k_ref,
    v_ref,
    g_ref,
    send_ref,
    base_ref,
    over_ref,
    header_ref,
    total_ref,
    columns_ref,
    arrived_ref,
):
    owners, send_rows, width = send_ref.shape
    tok_rows = q_ref.shape[0]
    head_size = width // 4
    step = pl.program_id(0)

    steps = columns_ref.shape[0]

    def column_copy(at_step, which):
        lanes = pl.ds((first_head + 2 * at_step) * head_size, 2 * head_size)
        return pltpu.make_async_copy(
            (q_ref, k_ref, v_ref, g_ref)[which].at[:, lanes],
            columns_ref.at[at_step, which],
            arrived_ref.at[at_step, which],
        )

    @pl.when(step == 0)
    def _():
        for at_step in range(steps):
            for which in range(4):
                column_copy(at_step, which).start()
        find_rows(first_head, ids_ref, slot_ref, base_ref, over_ref, header_ref)

    for at_step in range(steps):

        @pl.when(step == at_step)
        def _():
            for which in range(4):
                column_copy(at_step, which).wait()

    rows = [token_rows(columns_ref, step, at, head_size) for at in range(2)]
    halves = []
    for at in range(2):
        place = iota((owners * SHARED, tok_rows), 0) == base_ref[step * 2 + at]
        placed = dot(jnp.where(place, 1.0, 0.0).astype(BF16), rows[at])
        halves.append(placed.reshape(owners, SHARED, width))
    at_row = pl.multiple_of(step * 2 * SHARED, 2 * SHARED)
    shared = jnp.concatenate(halves, axis=1).astype(BF16)
    send_ref[:, pl.ds(at_row, 2 * SHARED), :] = shared

    places = [
        jnp.where(iota((owners * PACKED, tok_rows), 0) == over_ref[step * 2 + at], 1.0, 0.0).astype(BF16)
        for at in range(2)
    ]
    added = dot(jnp.concatenate(places, axis=1), jnp.concatenate(rows, axis=0))

    @pl.when(step == 0)
    def _():
        total_ref[...] = added

    @pl.when(step == pl.num_programs(0) - 1)
    def _():
        total = total_ref[...] + added
        last_row = iota((owners * PACKED, owners), 1) * PACKED + PACKED - 1
        to_last = jnp.where(iota((owners * PACKED, owners), 0) == last_row, 1.0, 0.0)
        tags = dot(to_last.astype(BF16), header_ref[...])
        total = jnp.concatenate([total[:, :head_size] + tags, total[:, head_size:]], axis=1)
        packed = total.astype(BF16).reshape(owners, PACKED, width)
        send_ref[:, send_rows - PACKED :, :] = packed


def own_rows_kernel(
    first_head,
    me_ref,
    shared_ref,
    over_ref,
    back_ref,
    peak_ref,
    turn_ref,
    causal_ref,
    rows_ref,
    grads_ref,
    sums_ref,
):
    sources, pair_rows, width = shared_ref.shape
    head_size = width // 4
    problems = rows_ref.shape[0]
    owned = problems // 2
    slot_count = sources * CAP
    bunch = 16
    groups = sources // bunch
    part = bunch * CAP
    shared_count = bunch * pair_rows
    packed_count = bunch * PACKED
    score_scale = 1.0 / math.sqrt(head_size)
    step = pl.program_id(0)
    steps = pl.num_programs(0)

    @pl.when(step == 0)
    def _():
        at = iota((slot_count, slot_count), 0)
        causal_ref[...] = jnp.where(iota((slot_count, slot_count), 1) <= at, 0.0, MASKED)

    header_of = jnp.where(
        iota((bunch, packed_count), 1) == iota((bunch, packed_count), 0) * PACKED + PACKED - 1,
        1.0,
        0.0,
    ).astype(BF16)

    def turns(header, first_lane, rows_each, used):
        count = bunch * rows_each
        lane = iota((head_size, count), 1) % rows_each
        match = (iota((head_size, count), 0) == lane + first_lane) & (lane < used)
        tags = dot(header, jnp.where(match, 1.0, 0.0).astype(BF16))
        source = iota((1, count), 1) // rows_each
        own = iota((bunch, count), 0) == source
        tag = jnp.sum(jnp.where(own, tags, 0.0), axis=0, keepdims=True).astype(jnp.int32) - 1
        mine = (tag >= 0) & (tag // (problems * CAP) == step)
        problem = (tag // CAP) % problems
        slot = jnp.where(mine, problem * part + source * CAP + tag % CAP, -1)
        hit = iota((problems * part, count), 0) == slot
        return jnp.where(hit, 1.0, 0.0).astype(BF16)

    ones = jnp.ones((shared_count + packed_count, head_size), BF16)
    peak_ref[...] = jnp.zeros(peak_ref.shape, F32)

    @pl.loop(0, groups)
    def _(group):
        from_sources = pl.ds(group * bunch, bunch)
        at_row = pl.multiple_of(group * part, part)
        packed = over_ref[from_sources].reshape(packed_count, width)
        shared = shared_ref[from_sources].reshape(shared_count, width)
        header = dot(header_of, packed[:, :head_size])
        peak_ref[...] = jnp.maximum(peak_ref[...], jnp.max(header, axis=0, keepdims=True))
        header = header.astype(BF16)
        turn = jnp.concatenate(
            [
                turns(header, step * pair_rows, pair_rows, pair_rows),
                turns(header, steps * pair_rows, PACKED, PACKED - SPARE),
            ],
            axis=1,
        )
        turn_ref[group] = turn
        turned = dot(turn, jnp.concatenate([shared, packed], axis=0))
        marked = turned[:, head_size : 2 * head_size] + (1.0 - dot(turn, ones)) * ABSENT
        turned = jnp.concatenate(
            [turned[:, :head_size], marked, turned[:, 2 * head_size :]], axis=1
        )
        rows_ref[:, pl.ds(at_row, part), :] = turned.astype(BF16).reshape(problems, part, width)

    first_lane = jnp.where(iota((8, head_size), 1) == 0, 1.0, 0.0).astype(BF16)

    def attend(problem):
        q = rows_ref[problem, :, 0:head_size]
        k = rows_ref[problem, :, head_size : 2 * head_size]
        v = rows_ref[problem, :, 2 * head_size : 3 * head_size]
        g = rows_ref[problem, :, 3 * head_size : 4 * head_size]
        marks = lax.dot_general(first_lane, k, CONTRACT_LAST, preferred_element_type=F32)
        present = marks < ABSENT / 2
        bias = jnp.where(present, 0.0, MASKED)[0:1]
        scores = lax.dot_general(q, k, CONTRACT_LAST, preferred_element_type=F32) * score_scale
        scores = scores + (causal_ref[...] + bias)
        weights = jnp.exp(scores - jnp.max(scores, axis=-1, keepdims=True))
        probs = weights / jnp.sum(weights, axis=-1, keepdims=True)
        probs_low = probs.astype(BF16)
        out = dot(probs_low, v).astype(BF16)
        grad_prob = lax.dot_general(g, v, CONTRACT_LAST, preferred_element_type=F32)
        delta = jnp.sum(g.astype(F32) * out.astype(F32), axis=-1, keepdims=True)
        grad_score = (probs * (grad_prob - delta) * score_scale).astype(BF16)
        grad_q = dot(grad_score, k)
        grad_k = lax.dot_general(grad_score, q, CONTRACT_FIRST, preferred_element_type=F32)
        grad_v = lax.dot_general(probs_low, g, CONTRACT_FIRST, preferred_element_type=F32)
        grads_ref[problem, :, 0:head_size] = out
        grads_ref[problem, :, head_size : 2 * head_size] = grad_q.astype(BF16)
        grads_ref[problem, :, 2 * head_size : 3 * head_size] = grad_k.astype(BF16)
        grads_ref[problem, :, 3 * head_size : 4 * head_size] = grad_v.astype(BF16)
        sums = dot(jnp.where(present, 1.0, 0.0).astype(BF16), k)[0:1]
        sums_ref[pl.ds(problem, 1), :] = sums

    @pl.loop(0, problems // 2)
    def _(pair):
        attend(pair * 2)
        attend(pair * 2 + 1)

    rest = slice(back_ref.shape[1] - PACKED, back_ref.shape[1])
    at_pair = pl.multiple_of(step * pair_rows, pair_rows)

    @pl.loop(0, groups)
    def _(group):
        from_sources = pl.ds(group * bunch, bunch)
        at_row = pl.multiple_of(group * part, part)
        leaving = grads_ref[:, pl.ds(at_row, part), :].reshape(problems * part, width)
        sent = lax.dot_general(
            turn_ref[group], leaving, CONTRACT_FIRST, preferred_element_type=F32
        ).astype(BF16)
        back_ref[from_sources, pl.ds(at_pair, pair_rows), :] = sent[:shared_count].reshape(
            bunch, pair_rows, width
        )
        packed = sent[shared_count:].reshape(bunch, PACKED, width)

        @pl.when(step == 0)
        def _():
            back_ref[from_sources, rest, :] = packed

        @pl.when(step > 0)
        def _():
            back_ref[from_sources, rest, :] += packed

    for at in range(2):
        sums = jnp.concatenate(
            [sums_ref[at * owned + slot : at * owned + slot + 1, :] for slot in range(owned)],
            axis=1,
        )
        high = sums.astype(BF16).astype(F32)
        low = sums - high
        turned_by = TURN_BY * (first_head + step * 2 + at)
        home = lax.rem(me_ref[0] + sources * TURN_BY - turned_by, sources)
        row = iota((PACKED, width), 0)
        tile = back_ref[home, rest, :].astype(F32)
        tile = jnp.where(row == PACKED - 2, high, jnp.where(row == PACKED - 1, low, tile))
        back_ref[home, rest, :] = tile.astype(BF16)


def unpack_rows_kernel(
    first_head, me_ref, base_ref, over_ref, cent_ref, shared_ref, packed_ref, *refs
):
    new_ref = refs[-1]
    out_refs = refs[-5:-1]
    owners, _, width = shared_ref.shape
    head_size = width // 4
    owned = cent_ref.shape[1]
    tok_rows, heads = base_ref.shape
    step = pl.program_id(0)
    packed = packed_ref[...].reshape(owners * PACKED, width)
    arrived = shared_ref[...].astype(F32)
    for at in range(2):
        here = iota((tok_rows, heads), 1) == step * 2 + at
        base = jnp.sum(jnp.where(here, base_ref[...], 0), axis=1, keepdims=True)
        over = jnp.sum(jnp.where(here, over_ref[...], 0), axis=1, keepdims=True)
        take = iota((tok_rows, owners * SHARED), 1) == base
        take_over = iota((tok_rows, owners * PACKED), 1) == over
        mine = arrived[:, at * SHARED : (at + 1) * SHARED, :].reshape(owners * SHARED, width)
        rows = dot(jnp.where(take, 1.0, 0.0).astype(BF16), mine.astype(BF16))
        rows = rows + dot(jnp.where(take_over, 1.0, 0.0).astype(BF16), packed)
        rows = rows.astype(BF16)
        for which, out_ref in enumerate(out_refs):
            out_ref[:, at * head_size : (at + 1) * head_size] = rows[
                :, which * head_size : (which + 1) * head_size
            ]
        turned_by = TURN_BY * (first_head + step * 2 + at)
        tile = packed_ref[lax.rem(me_ref[0] + turned_by, owners)].astype(F32)
        spare = iota((PACKED, width), 0) >= PACKED - 2
        key_sums = jnp.sum(jnp.where(spare, tile, 0.0), axis=0, keepdims=True)
        for slot in range(owned):
            blend = DECAY_RATE * cent_ref[at, slot : slot + 1, :]
            blend += (1.0 - DECAY_RATE) * key_sums[:, slot * head_size : (slot + 1) * head_size]
            new_ref[at, slot : slot + 1, :] = blend / jnp.sqrt(
                jnp.mean(blend * blend, axis=-1, keepdims=True) + 1e-06
            )


def params(limit=VMEM_BYTES):
    return pltpu.CompilerParams(vmem_limit_bytes=limit)


def dense(queries, keys, values, out_grad, cluster_ids, cluster_slot, centroids):
    seq_count = lax.axis_size("seq")
    local_heads, tok_rows = cluster_ids.shape[:2]
    cluster_count = cluster_slot.shape[0]
    owned = cluster_count // seq_count
    head_size = centroids.shape[2]
    heads = local_heads
    block_rows = owned * CAP
    width = 4 * head_size
    slot_count = seq_count * CAP
    sent = jax.ShapeDtypeStruct((seq_count, heads * block_rows, width), BF16)
    sent_bytes = seq_count * heads * block_rows * width * 2
    ids_rows = cluster_ids.reshape(local_heads, 1, tok_rows)
    slot_row = cluster_slot.reshape(1, cluster_count)
    block = pl.BlockSpec((seq_count, block_rows, width), lambda h: (0, h, 0))

    def exchange(rows):
        return lax.all_to_all(rows, "seq", split_axis=0, concat_axis=0, tiled=True)

    def pack(chunk):
        column = pl.BlockSpec((tok_rows, head_size), lambda h: (0, chunk * heads + h))
        return pl.pallas_call(
            pack_kernel,
            grid=(heads,),
            in_specs=[
                pl.BlockSpec((1, 1, tok_rows), lambda h: (chunk * heads + h, 0, 0)),
                pl.BlockSpec((1, cluster_count), lambda h: (0, 0)),
                column,
                column,
                column,
                column,
            ],
            out_specs=[block, pl.BlockSpec((1, 1, tok_rows), lambda h: (h, 0, 0))],
            out_shape=[sent, jax.ShapeDtypeStruct((heads, 1, tok_rows), jnp.int32)],
            scratch_shapes=[pltpu.VMEM((tok_rows, tok_rows), BF16)],
            compiler_params=params(),
            cost_estimate=pl.CostEstimate(
                flops=heads * 2 * 1024 * 512 * 640, bytes_accessed=2 * sent_bytes, transcendentals=0
            ),
            name="pack",
        )(ids_rows, slot_row, queries, keys, values, out_grad)

    def own(chunk, received):
        return pl.pallas_call(
            owner_kernel,
            grid=(heads,),
            in_specs=[
                block,
                pl.BlockSpec((1, owned, head_size), lambda h: (chunk * heads + h, 0, 0)),
            ],
            out_specs=[block, pl.BlockSpec((1, owned, head_size), lambda h: (h, 0, 0))],
            out_shape=[sent, jax.ShapeDtypeStruct((heads, owned, head_size), F32)],
            scratch_shapes=[
                pltpu.VMEM((16 * block_rows, 16 * block_rows), BF16),
                pltpu.VMEM((slot_count, slot_count), F32),
                pltpu.VMEM((owned, slot_count, width), BF16),
                pltpu.VMEM((owned, slot_count, width), BF16),
            ],
            compiler_params=params(),
            cost_estimate=pl.CostEstimate(
                flops=heads * owned * 7 * 2 * slot_count * slot_count * head_size,
                bytes_accessed=2 * sent_bytes,
                transcendentals=heads * owned * slot_count * slot_count,
            ),
            name="own",
        )(received, centroids)

    def unpack(chunk, flat_cols, returned, previous):
        column = pl.BlockSpec((tok_rows, head_size), lambda h: (0, chunk * heads + h))
        whole = jax.ShapeDtypeStruct((tok_rows, local_heads * head_size), BF16)

        def kernel(*refs):
            unpack_kernel(chunk, *refs)

        return pl.pallas_call(
            kernel,
            grid=(heads,),
            in_specs=[pl.BlockSpec((tok_rows, heads), lambda h: (0, 0)), block]
            + [pl.BlockSpec(memory_space=pl.ANY)] * len(previous),
            out_specs=[column] * 4,
            out_shape=[whole] * 4,
            input_output_aliases={2 + i: i for i in range(len(previous))},
            compiler_params=params(),
            cost_estimate=pl.CostEstimate(
                flops=heads * 2 * 1024 * 512 * 512, bytes_accessed=2 * sent_bytes, transcendentals=0
            ),
            name="unpack",
        )(flat_cols, returned, *previous)

    packed = [pack(chunk) for chunk in range(1)]
    received = [exchange(rows) for rows, _ in packed]
    owned_now = [own(chunk, rows) for chunk, rows in enumerate(received)]
    returned = [exchange(rows) for rows, _ in owned_now]
    outs = ()
    for chunk in range(1):
        flat_cols = packed[chunk][1].reshape(heads, tok_rows).T
        outs = unpack(chunk, flat_cols, returned[chunk], tuple(outs))
    new_centroids = jnp.concatenate([new for _, new in owned_now], axis=0)
    return (*outs, new_centroids)


def body(queries, keys, values, out_grad, cluster_ids, cluster_slot, centroids):
    seq_count = lax.axis_size("seq")
    local_heads, tok_rows = cluster_ids.shape[:2]
    cluster_count = cluster_slot.shape[0]
    owned, head_size = centroids.shape[1:]
    heads = local_heads // CHUNKS
    width = 4 * head_size
    pair_rows = 2 * SHARED
    steps = heads // 2
    send_rows = steps * pair_rows + PACKED
    slot_count = seq_count * CAP
    problems = 2 * owned
    block_bytes = seq_count * pair_rows * width * 2
    sent_shape = jax.ShapeDtypeStruct((seq_count, send_rows, width), BF16)
    ids_rows = cluster_ids.reshape(local_heads, 1, tok_rows)
    slot_row = cluster_slot.reshape(1, cluster_count)
    me = lax.axis_index("seq").reshape(1)

    def cost(flops, exps=0):
        return pl.CostEstimate(
            flops=flops, bytes_accessed=2 * (steps + 1) * block_bytes, transcendentals=exps
        )

    shared_block = pl.BlockSpec((seq_count, pair_rows, width), lambda s: (0, s, 0))
    packed_block = pl.BlockSpec((seq_count, PACKED, width), lambda s: (0, steps, 0))
    whole_block = pl.BlockSpec((seq_count, send_rows, width), lambda s: (0, 0, 0))
    me_spec = pl.BlockSpec(memory_space=pltpu.SMEM)

    def pack(chunk):
        row_shape = jax.ShapeDtypeStruct((heads, 1, tok_rows), jnp.int32)
        rows_block = pl.BlockSpec((heads, 1, tok_rows), lambda s: (0, 0, 0))
        return pl.pallas_call(
            functools.partial(pack_rows_kernel, chunk * heads),
            grid=(steps,),
            in_specs=[
                pl.BlockSpec((heads, 1, tok_rows), lambda s: (chunk, 0, 0)),
                pl.BlockSpec((1, cluster_count), lambda s: (0, 0)),
            ]
            + [pl.BlockSpec(memory_space=pl.ANY)] * 4,
            out_specs=[whole_block, rows_block, rows_block],
            out_shape=[sent_shape, row_shape, row_shape],
            scratch_shapes=[
                pltpu.VMEM((seq_count, head_size), BF16),
                pltpu.VMEM((seq_count * PACKED, width), F32),
                pltpu.VMEM((steps, 4, tok_rows, 2 * head_size), BF16),
                pltpu.SemaphoreType.DMA((steps, 4)),
            ],
            compiler_params=params(),
            cost_estimate=cost(2 * heads * 1536 * tok_rows * width),
            name="pack_rows",
        )(ids_rows, slot_row, queries, keys, values, out_grad)

    def own(chunk, received):
        return pl.pallas_call(
            functools.partial(own_rows_kernel, chunk * heads),
            grid=(steps,),
            in_specs=[me_spec, shared_block, packed_block],
            out_specs=[whole_block, pl.BlockSpec((8, head_size), lambda s: (0, 0))],
            out_shape=[sent_shape, jax.ShapeDtypeStruct((8, head_size), F32)],
            scratch_shapes=[
                pltpu.VMEM(
                    (seq_count // 16, problems * 16 * CAP, 16 * (pair_rows + PACKED)), BF16
                ),
                pltpu.VMEM((slot_count, slot_count), F32),
                pltpu.VMEM((problems, slot_count, width), BF16),
                pltpu.VMEM((problems, slot_count, width), BF16),
                pltpu.VMEM((problems, head_size), F32),
            ],
            compiler_params=params(),
            cost_estimate=cost(
                steps * problems * 16 * 2 * slot_count * slot_count * head_size,
                steps * problems * slot_count * slot_count,
            ),
            name="own_rows",
        )(me, received, received)

    def unpack(chunk, base_rows, over_rows, returned, previous):
        column = pl.BlockSpec((tok_rows, 2 * head_size), lambda s: (0, chunk * steps + s))
        routes_block = pl.BlockSpec((tok_rows, heads), lambda s: (0, 0))
        centroid_block = pl.BlockSpec(
            (2, owned, head_size), lambda s: (chunk * steps + s, 0, 0)
        )
        return pl.pallas_call(
            functools.partial(unpack_rows_kernel, chunk * heads),
            grid=(steps,),
            in_specs=[
                me_spec,
                routes_block,
                routes_block,
                centroid_block,
                shared_block,
                packed_block,
            ]
            + [pl.BlockSpec(memory_space=pl.ANY)] * len(previous),
            out_specs=[column] * 4 + [centroid_block],
            out_shape=[pltpu.HBM((tok_rows, local_heads * head_size), BF16)] * 4
            + [pltpu.HBM(centroids.shape, F32)],
            input_output_aliases={6 + at: at for at in range(len(previous))},
            compiler_params=params(LESS_VMEM_BYTES),
            cost_estimate=cost(2 * heads * 1536 * tok_rows * width),
            name="unpack_rows",
        )(
            me,
            base_rows.reshape(heads, tok_rows).T,
            over_rows.reshape(heads, tok_rows).T,
            centroids,
            returned,
            returned,
            *previous,
        )

    def exchange(rows):
        return lax.all_to_all(rows, "seq", split_axis=0, concat_axis=0, tiled=True)

    packed = [pack(chunk) for chunk in range(CHUNKS)]
    received = [exchange(rows) for rows, _, _ in packed]
    owned_now = [own(chunk, received[chunk]) for chunk in range(CHUNKS)]
    returned = [exchange(back) for back, _ in owned_now]
    outs = ()
    for chunk in range(CHUNKS):
        outs = unpack(chunk, *packed[chunk][1:], returned[chunk], tuple(outs))

    peak = functools.reduce(jnp.maximum, [seen[0:1] for _, seen in owned_now])
    swap = [(at, 1 - at) for at in range(2)]
    peak = jnp.maximum(peak, lax.ppermute(peak, "head", swap))[0, PEAK_LANE]

    def lacking(state):
        return state[0]

    def again(state):
        full = dense(queries, keys, values, out_grad, cluster_ids, cluster_slot, centroids)
        return (jnp.zeros((), jnp.bool_), *full)

    state = lax.while_loop(lacking, again, (peak > PACKED - SPARE, *outs))
    return state[1:]


def solution(mesh):
    return jax.shard_map(
        body,
        mesh=mesh,
        in_specs=(
            P("seq", "head"),
            P("seq", "head"),
            P("seq", "head"),
            P("seq", "head"),
            P("head", "seq", None),
            P(),
            P("head", "seq", None),
        ),
        out_specs=(
            P("seq", "head"),
            P("seq", "head"),
            P("seq", "head"),
            P("seq", "head"),
            P("head", "seq", None),
        ),
        check_vma=False,
    )
```

profile of v0, /device:TPU:0, one launch (start us, length us, event | category | flops | bytes accessed | tf_op | source)
XLA Modules:
  0.0 205.6 jit_solution(10377762357925479497)
XLA Ops:
  0.6 8.2 %pack_rows.2 = (bf16[64,48,512]{2,1,0:T(8,128)(2,1)}, s32[4,1,512]{2,1,0:T(1,128)}, s32[4,1,512]{2,1,0:T(1,128)}) custom-call(s32[8,1,512]{2,1,0:T(1,128)} %bitcast.26, s32[1,256]{1,0:T(1,128)} %bitcast.29, bf16[512,1024]{1,0:T(8,128)(2,1)} %q_ref.3, bf16[512,1024]{1,0:T(8,128)(2,1)} %k_ref.3, bf16[512,1024]{1,0:T(8,128)(2,1)} %v_ref.3, bf16[512,1024]{1,0:T(8,128)(2,1)} %g_ref.3), custom_call_target="tpu_custom_call" | custom-call | flops 3221225472 | bytes 6291456 | tf_op jit(solution)/shard_map/pack_rows/pallas_call | solution.py:612
  8.8 0.0 copy-start.8
  8.9 0.0 copy-start.10
  8.9 11.7 %all-to-all-start.2 = ((bf16[64,48,512]{2,1,0:T(8,128)(2,1)}), bf16[64,48,512]{2,1,0:T(8,128)(2,1)}, u32[]{:S(2)}, u32[]{:S(2)}) async-start(bf16[64,48,512]{2,1,0:T(8,128)(2,1)} %get-tuple-element.98), calls=%async_computation.2 | async-start | bytes 6291456 | tf_op jit(solution)/shard_map/all_to_all | solution.py:693
  20.6 0.0 copy-done.8
  20.6 0.0 copy-done.10
  20.6 7.6 %pack_rows.3 = (bf16[64,48,512]{2,1,0:T(8,128)(2,1)}, s32[4,1,512]{2,1,0:T(1,128)}, s32[4,1,512]{2,1,0:T(1,128)}) custom-call(s32[8,1,512]{2,1,0:T(1,128)S(1)} %bitcast.27, s32[1,256]{1,0:T(1,128)S(1)} %bitcast.30, bf16[512,1024]{1,0:T(8,128)(2,1)} %q_ref.3, bf16[512,1024]{1,0:T(8,128)(2,1)} %k_ref.3, bf16[512,1024]{1,0:T(8,128)(2,1)} %v_ref.3, ...), custom_call_target="tpu_custom_call" | custom-call | flops 3221225472 | bytes 6291456 | tf_op jit(solution)/shard_map/pack_rows/pallas_call | solution.py:612
  28.2 32.8 %all-to-all-done.2.shared_ref.over_ref = bf16[64,48,512]{2,1,0:T(8,128)(2,1)} async-done(((bf16[64,48,512]{2,1,0:T(8,128)(2,1)}), bf16[64,48,512]{2,1,0:T(8,128)(2,1)}, u32[]{:S(2)}, u32[]{:S(2)}) %all-to-all-start.2) | async-done | bytes 3145760 | tf_op jit(solution)/shard_map/all_to_all | solution.py:693
  61.0 9.2 %all-to-all-start.3 = ((bf16[64,48,512]{2,1,0:T(8,128)(2,1)}), bf16[64,48,512]{2,1,0:T(8,128)(2,1)}, u32[]{:S(2)}, u32[]{:S(2)}) async-start(bf16[64,48,512]{2,1,0:T(8,128)(2,1)} %get-tuple-element.100), calls=%async_computation.3 | async-start | bytes 6291456 | tf_op jit(solution)/shard_map/all_to_all | solution.py:693
  70.2 27.8 %own_rows.2 = (bf16[64,48,512]{2,1,0:T(8,128)(2,1)}, f32[8,128]{1,0:T(8,128)}) custom-call(s32[1]{0:T(128)} %bitcast.5.me_ref, bf16[64,48,512]{2,1,0:T(8,128)(2,1)} %all-to-all-done.2.shared_ref.over_ref, bf16[64,48,512]{2,1,0:T(8,128)(2,1)} %all-to-all-done.2.shared_ref.over_ref), custom_call_target="tpu_custom_call" | custom-call | flops 4294967296 | bytes 6291456 | tf_op jit(solution)/shard_map/own_rows/pallas_call | solution.py:634
  98.0 10.8 %all-to-all-done.3.shared_ref.over_ref = bf16[64,48,512]{2,1,0:T(8,128)(2,1)} async-done(((bf16[64,48,512]{2,1,0:T(8,128)(2,1)}), bf16[64,48,512]{2,1,0:T(8,128)(2,1)}, u32[]{:S(2)}, u32[]{:S(2)}) %all-to-all-start.3) | async-done | bytes 3145760 | tf_op jit(solution)/shard_map/all_to_all | solution.py:693
  108.8 6.5 %all-to-all-start.5 = ((bf16[64,48,512]{2,1,0:T(8,128)(2,1)}), bf16[64,48,512]{2,1,0:T(8,128)(2,1)}, u32[]{:S(2)}, u32[]{:S(2)}) async-start(bf16[64,48,512]{2,1,0:T(8,128)(2,1)} %get-tuple-element.107), calls=%async_computation.5 | async-start | bytes 6291456 | tf_op jit(solution)/shard_map/all_to_all | solution.py:693
  115.3 27.8 %own_rows.3 = (bf16[64,48,512]{2,1,0:T(8,128)(2,1)}, f32[8,128]{1,0:T(8,128)}) custom-call(s32[1]{0:T(128)} %bitcast.5.me_ref, bf16[64,48,512]{2,1,0:T(8,128)(2,1)} %all-to-all-done.3.shared_ref.over_ref, bf16[64,48,512]{2,1,0:T(8,128)(2,1)} %all-to-all-done.3.shared_ref.over_ref), custom_call_target="tpu_custom_call" | custom-call | flops 4294967296 | bytes 6291456 | tf_op jit(solution)/shard_map/own_rows/pallas_call | solution.py:634
  143.1 11.3 %all-to-all-done.5.shared_ref.packed_ref = bf16[64,48,512]{2,1,0:T(8,128)(2,1)} async-done(((bf16[64,48,512]{2,1,0:T(8,128)(2,1)}), bf16[64,48,512]{2,1,0:T(8,128)(2,1)}, u32[]{:S(2)}, u32[]{:S(2)}) %all-to-all-start.5) | async-done | bytes 3145760 | tf_op jit(solution)/shard_map/all_to_all | solution.py:693
  154.4 0.0 copy-start.9
  154.4 6.1 %all-to-all-start.4 = ((bf16[64,48,512]{2,1,0:T(8,128)(2,1)}), bf16[64,48,512]{2,1,0:T(8,128)(2,1)S(1)}, u32[]{:S(2)}, u32[]{:S(2)}) async-start(bf16[64,48,512]{2,1,0:T(8,128)(2,1)} %get-tuple-element.104), calls=%async_computation.4 | async-start | bytes 6291456 | tf_op jit(solution)/shard_map/all_to_all | solution.py:693
  160.5 0.7 slice_maximum_fusion
  161.2 0.0 collective-permute-start
  161.2 0.0 copy-done.5
  161.2 0.9 copy.20
  162.1 0.9 copy.21
  162.9 0.1 copy.18
  163.1 0.9 copy.19
  164.0 0.0 collective-permute-done
  164.0 0.6 slice.11
  165.2 0.0 copy-start.1
  165.2 0.9 copy-done.1
  166.2 0.9 copy-done.2
  167.1 6.7 %unpack_rows.2 = (bf16[512,1024]{1,0:T(8,128)(2,1)}, bf16[512,1024]{1,0:T(8,128)(2,1)}, bf16[512,1024]{1,0:T(8,128)(2,1)}, bf16[512,1024]{1,0:T(8,128)(2,1)}, f32[8,4,128]{2,1,0:T(4,128)}) custom-call(s32[1]{0:T(128)} %bitcast.5.me_ref, s32[512,4]{1,0:T(8,128)S(1)} %bitcast.23, s32[512,4]{1,0:T(8,128)S(1)} %bitcast.24, f32[8,4,128]{2,1,0:T(4,128)S(1)} %copy-done.9, ...), custom_call_target="tpu_custom_call" | custom-call | flops 3221225472 | bytes 6291456 | tf_op jit(solution)/shard_map/unpack_rows/pallas_call | solution.py:663
  173.8 25.4 %all-to-all-done.4.shared_ref.packed_ref = bf16[64,48,512]{2,1,0:T(8,128)(2,1)S(1)} async-done(((bf16[64,48,512]{2,1,0:T(8,128)(2,1)}), bf16[64,48,512]{2,1,0:T(8,128)(2,1)S(1)}, u32[]{:S(2)}, u32[]{:S(2)}) %all-to-all-start.4) | async-done | bytes 3145760 | tf_op jit(solution)/shard_map/all_to_all | solution.py:693
  199.3 0.9 copy-done
  200.2 5.4 %unpack_rows.3 = (bf16[512,1024]{1,0:T(8,128)(2,1)}, bf16[512,1024]{1,0:T(8,128)(2,1)}, bf16[512,1024]{1,0:T(8,128)(2,1)}, bf16[512,1024]{1,0:T(8,128)(2,1)}, f32[8,4,128]{2,1,0:T(4,128)}) custom-call(s32[1]{0:T(128)} %bitcast.5.me_ref, s32[512,4]{1,0:T(8,128)S(1)} %bitcast.21, ...), custom_call_target="tpu_custom_call", output_to_operand_aliasing={{0}: (6, {}), {1}: (7, {}), {2}: (8, {}), {3}: (9, {}), {4}... | custom-call | flops 3221225472 | bytes 6291456 | tf_op jit(solution)/shard_map/unpack_rows/pallas_call | solution.py:663
  (12 shorter events, 0.0 us)
Async XLA Ops:
  8.8 11.8 %copy-start.8 = (s32[8,512,1]{1,2,0:T(1,128)S(1)}, s32[8,512,1]{1,2,0:T(1,128)}, u32[]{:S(2)}) copy-start(s32[8,512,1]{1,2,0:T(1,128)} %param.13) | copy-start | bytes 49156
  8.9 11.8 %copy-start.10 = (s32[256]{0:T(256)S(1)}, s32[256]{0:T(256)}, u32[]{:S(2)}) copy-start(s32[256]{0:T(256)} %param.14) | copy-start | bytes 3076
  8.9 52.1 %all-to-all-start.2 = ((bf16[64,48,512]{2,1,0:T(8,128)(2,1)}), bf16[64,48,512]{2,1,0:T(8,128)(2,1)}, u32[]{:S(2)}, u32[]{:S(2)}) async-start(bf16[64,48,512]{2,1,0:T(8,128)(2,1)} %get-tuple-element.98), calls=%async_computation.2 | async-start | bytes 6291456 | tf_op jit(solution)/shard_map/all_to_all | solution.py:693
  61.0 47.8 %all-to-all-start.3 = ((bf16[64,48,512]{2,1,0:T(8,128)(2,1)}), bf16[64,48,512]{2,1,0:T(8,128)(2,1)}, u32[]{:S(2)}, u32[]{:S(2)}) async-start(bf16[64,48,512]{2,1,0:T(8,128)(2,1)} %get-tuple-element.100), calls=%async_computation.3 | async-start | bytes 6291456 | tf_op jit(solution)/shard_map/all_to_all | solution.py:693
  108.8 45.6 %all-to-all-start.5 = ((bf16[64,48,512]{2,1,0:T(8,128)(2,1)}), bf16[64,48,512]{2,1,0:T(8,128)(2,1)}, u32[]{:S(2)}, u32[]{:S(2)}) async-start(bf16[64,48,512]{2,1,0:T(8,128)(2,1)} %get-tuple-element.107), calls=%async_computation.5 | async-start | bytes 6291456 | tf_op jit(solution)/shard_map/all_to_all | solution.py:693
  154.4 6.9 %copy-start.5 = (s32[4,1,512]{2,1,0:T(1,128)S(1)}, s32[4,1,512]{2,1,0:T(1,128)}, u32[]{:S(2)}) copy-start(s32[4,1,512]{2,1,0:T(1,128)} %get-tuple-element.105) | copy-start | bytes 24580
  154.4 7.7 %copy-start.4 = (s32[4,1,512]{2,1,0:T(1,128)S(1)}, s32[4,1,512]{2,1,0:T(1,128)}, u32[]{:S(2)}) copy-start(s32[4,1,512]{2,1,0:T(1,128)} %get-tuple-element.106) | copy-start | bytes 24580
  154.4 8.6 %copy-start.7 = (s32[4,1,512]{2,1,0:T(1,128)S(1)}, s32[4,1,512]{2,1,0:T(1,128)}, u32[]{:S(2)}) copy-start(s32[4,1,512]{2,1,0:T(1,128)} %get-tuple-element.102) | copy-start | bytes 24580
  154.4 8.7 %copy-start.6 = (s32[4,1,512]{2,1,0:T(1,128)S(1)}, s32[4,1,512]{2,1,0:T(1,128)}, u32[]{:S(2)}) copy-start(s32[4,1,512]{2,1,0:T(1,128)} %get-tuple-element.103) | copy-start | bytes 24580
  154.4 10.8 %copy-start.9 = (f32[8,4,128]{2,1,0:T(4,128)S(1)}, f32[8,4,128]{2,1,0:T(4,128)}, u32[]{:S(2)}) copy-start(f32[8,4,128]{2,1,0:T(4,128)} %cent_ref.3) | copy-start | bytes 49156
  154.4 44.9 %all-to-all-start.4 = ((bf16[64,48,512]{2,1,0:T(8,128)(2,1)}), bf16[64,48,512]{2,1,0:T(8,128)(2,1)S(1)}, u32[]{:S(2)}, u32[]{:S(2)}) async-start(bf16[64,48,512]{2,1,0:T(8,128)(2,1)} %get-tuple-element.104), calls=%async_computation.4 | async-start | bytes 6291456 | tf_op jit(solution)/shard_map/all_to_all | solution.py:693
  161.2 2.8 %collective-permute-start = (f32[1,128]{1,0:T(1,128)S(1)}, f32[1,128]{1,0:T(1,128)S(1)}, u32[]{:S(2)}, u32[]{:S(2)}) collective-permute-start(f32[1,128]{1,0:T(1,128)S(1)} %slice_maximum_fusion), channel_id=1, source_target_pairs={{0,1},{1,0},{2,3},{3,2},{4,5},{5,4},{6,7},{7,6},{8,9},{9,8},{10,11... | collective-permute-start | bytes 1544 | tf_op jit(solution)/shard_map/ppermute | solution.py:705
  165.2 1.0 copy-start.1
  166.2 0.9 copy-start.2
  199.3 1.0 copy-start
where the time goes:
time: 206 us
  Pallas kernels  83.5 us (41%)
  waiting for transfers between devices  80.3 us (39%)
  starting transfers between devices  33.5 us (16%)
  local copies, waits for them, and re-layouts  6.19 us (3%)
    all_to_all x4, waiting for transfers between devices, exchange(): return lax.all_to_all(rows, 'seq', split_axis=0, concat_axis=0, tiled=True)  80.3 us
    pallas_call x2, Pallas kernels, own(): pl.pallas_call(functools.partial(own_rows_kernel, chunk * heads), grid=(s...  55.6 us
    all_to_all x4, starting transfers between devices, exchange(): return lax.all_to_all(rows, 'seq', split_axis=0, concat_axis=0, tiled=True)  33.5 us
    pallas_call x2, Pallas kernels, pack(): pl.pallas_call(functools.partial(pack_rows_kernel, chunk * heads), grid=(...  15.8 us
    pallas_call x2, Pallas kernels, unpack(): pl.pallas_call(functools.partial(unpack_rows_kernel, chunk * heads), grid...  12.1 us
  transfers between devices with their start and end apart: 5, of which 4 were waited for; matrix products, arithmetic and copies ran while one was open for 2% of the time, Pallas kernels for 34%

commit v1 on v0

--- a/solution.py
+++ b/solution.py
@@ -681,8 +681,8 @@
             name="unpack_rows",
         )(
             me,
-            base_rows.reshape(heads, tok_rows).T,
-            over_rows.reshape(heads, tok_rows).T,
+            pltpu.with_memory_space_constraint(base_rows.reshape(heads, tok_rows).T, pltpu.HBM),
+            pltpu.with_memory_space_constraint(over_rows.reshape(heads, tok_rows).T, pltpu.HBM),
             centroids,
             returned,
             returned,

time: 206 us -> 207 us (level)
  local copies, waits for them, and re-layouts: 6.19 us -> 4.05 us
    unnamed x20 -> x14, local copies, waits for them, and re-layouts: 2.88 us -> 0.03 us
where the time goes in v1:
time: 207 us; the launch traced here: 206 us
  Pallas kernels  84.6 us (41%)
  waiting for transfers between devices  81.4 us (39%)
  starting transfers between devices  33.5 us (16%)
  local copies, waits for them, and re-layouts  4.05 us (2%)
    all_to_all x4, waiting for transfers between devices, exchange(): return lax.all_to_all(rows, 'seq', split_axis=0, concat_axis=0, tiled=True)  81.4 us
    pallas_call x2, Pallas kernels, own(): pl.pallas_call(functools.partial(own_rows_kernel, chunk * heads), grid=(s...  55.6 us
    all_to_all x4, starting transfers between devices, exchange(): return lax.all_to_all(rows, 'seq', split_axis=0, concat_axis=0, tiled=True)  33.5 us
    pallas_call x2, Pallas kernels, pack(): pl.pallas_call(functools.partial(pack_rows_kernel, chunk * heads), grid=(...  15.8 us
    pallas_call x2, Pallas kernels, unpack(): pl.pallas_call(functools.partial(unpack_rows_kernel, chunk * heads), grid...  13.2 us
  transfers between devices with their start and end apart: 5, of which 4 were waited for; matrix products, arithmetic and copies ran while one was open for 2% of the time, Pallas kernels for 34%

profile of v1, /device:TPU:0, one launch (start us, length us, event | category | flops | bytes accessed | tf_op | source)
XLA Modules:
  0.0 205.8 jit_solution(16321044288517570231)
XLA Ops:
  0.6 8.3 %pack_rows.2 = (bf16[64,48,512]{2,1,0:T(8,128)(2,1)}, s32[4,1,512]{2,1,0:T(1,128)}, s32[4,1,512]{2,1,0:T(1,128)}) custom-call(s32[8,1,512]{2,1,0:T(1,128)} %bitcast.26, s32[1,256]{1,0:T(1,128)} %bitcast.29, bf16[512,1024]{1,0:T(8,128)(2,1)} %q_ref.3, bf16[512,1024]{1,0:T(8,128)(2,1)} %k_ref.3, bf16[512,1024]{1,0:T(8,128)(2,1)} %v_ref.3, bf16[512,1024]{1,0:T(8,128)(2,1)} %g_ref.3), custom_call_target="tpu_custom_call" | custom-call | flops 3221225472 | bytes 6291456 | tf_op jit(solution)/shard_map/pack_rows/pallas_call | solution.py:612
  8.9 0.0 copy-start.5
  8.9 0.0 copy-start.7
  9.0 11.7 %all-to-all-start.2 = ((bf16[64,48,512]{2,1,0:T(8,128)(2,1)}), bf16[64,48,512]{2,1,0:T(8,128)(2,1)}, u32[]{:S(2)}, u32[]{:S(2)}) async-start(bf16[64,48,512]{2,1,0:T(8,128)(2,1)} %get-tuple-element.98), calls=%async_computation.2 | async-start | bytes 6291456 | tf_op jit(solution)/shard_map/all_to_all | solution.py:693
  20.7 0.0 copy-done.5
  20.7 0.0 copy-done.7
  20.7 7.5 %pack_rows.3 = (bf16[64,48,512]{2,1,0:T(8,128)(2,1)}, s32[4,1,512]{2,1,0:T(1,128)}, s32[4,1,512]{2,1,0:T(1,128)}) custom-call(s32[8,1,512]{2,1,0:T(1,128)S(1)} %bitcast.27, s32[1,256]{1,0:T(1,128)S(1)} %bitcast.30, bf16[512,1024]{1,0:T(8,128)(2,1)} %q_ref.3, bf16[512,1024]{1,0:T(8,128)(2,1)} %k_ref.3, bf16[512,1024]{1,0:T(8,128)(2,1)} %v_ref.3, ...), custom_call_target="tpu_custom_call" | custom-call | flops 3221225472 | bytes 6291456 | tf_op jit(solution)/shard_map/pack_rows/pallas_call | solution.py:612
  28.3 32.8 %all-to-all-done.2.shared_ref.over_ref = bf16[64,48,512]{2,1,0:T(8,128)(2,1)} async-done(((bf16[64,48,512]{2,1,0:T(8,128)(2,1)}), bf16[64,48,512]{2,1,0:T(8,128)(2,1)}, u32[]{:S(2)}, u32[]{:S(2)}) %all-to-all-start.2) | async-done | bytes 3145760 | tf_op jit(solution)/shard_map/all_to_all | solution.py:693
  61.1 9.2 %all-to-all-start.3 = ((bf16[64,48,512]{2,1,0:T(8,128)(2,1)}), bf16[64,48,512]{2,1,0:T(8,128)(2,1)}, u32[]{:S(2)}, u32[]{:S(2)}) async-start(bf16[64,48,512]{2,1,0:T(8,128)(2,1)} %get-tuple-element.100), calls=%async_computation.3 | async-start | bytes 6291456 | tf_op jit(solution)/shard_map/all_to_all | solution.py:693
  70.2 27.8 %own_rows.2 = (bf16[64,48,512]{2,1,0:T(8,128)(2,1)}, f32[8,128]{1,0:T(8,128)}) custom-call(s32[1]{0:T(128)} %bitcast.5.me_ref, bf16[64,48,512]{2,1,0:T(8,128)(2,1)} %all-to-all-done.2.shared_ref.over_ref, bf16[64,48,512]{2,1,0:T(8,128)(2,1)} %all-to-all-done.2.shared_ref.over_ref), custom_call_target="tpu_custom_call" | custom-call | flops 4294967296 | bytes 6291456 | tf_op jit(solution)/shard_map/own_rows/pallas_call | solution.py:634
  98.0 10.8 %all-to-all-done.3.shared_ref.over_ref = bf16[64,48,512]{2,1,0:T(8,128)(2,1)} async-done(((bf16[64,48,512]{2,1,0:T(8,128)(2,1)}), bf16[64,48,512]{2,1,0:T(8,128)(2,1)}, u32[]{:S(2)}, u32[]{:S(2)}) %all-to-all-start.3) | async-done | bytes 3145760 | tf_op jit(solution)/shard_map/all_to_all | solution.py:693
  108.9 6.5 %all-to-all-start.5 = ((bf16[64,48,512]{2,1,0:T(8,128)(2,1)}), bf16[64,48,512]{2,1,0:T(8,128)(2,1)}, u32[]{:S(2)}, u32[]{:S(2)}) async-start(bf16[64,48,512]{2,1,0:T(8,128)(2,1)} %get-tuple-element.107), calls=%async_computation.5 | async-start | bytes 6291456 | tf_op jit(solution)/shard_map/all_to_all | solution.py:693
  115.4 27.8 %own_rows.3 = (bf16[64,48,512]{2,1,0:T(8,128)(2,1)}, f32[8,128]{1,0:T(8,128)}) custom-call(s32[1]{0:T(128)} %bitcast.5.me_ref, bf16[64,48,512]{2,1,0:T(8,128)(2,1)} %all-to-all-done.3.shared_ref.over_ref, bf16[64,48,512]{2,1,0:T(8,128)(2,1)} %all-to-all-done.3.shared_ref.over_ref), custom_call_target="tpu_custom_call" | custom-call | flops 4294967296 | bytes 6291456 | tf_op jit(solution)/shard_map/own_rows/pallas_call | solution.py:634
  143.1 11.3 %all-to-all-done.5.shared_ref.packed_ref = bf16[64,48,512]{2,1,0:T(8,128)(2,1)} async-done(((bf16[64,48,512]{2,1,0:T(8,128)(2,1)}), bf16[64,48,512]{2,1,0:T(8,128)(2,1)}, u32[]{:S(2)}, u32[]{:S(2)}) %all-to-all-start.5) | async-done | bytes 3145760 | tf_op jit(solution)/shard_map/all_to_all | solution.py:693
  154.5 0.0 copy-start.6
  154.5 6.1 %all-to-all-start.4 = ((bf16[64,48,512]{2,1,0:T(8,128)(2,1)}), bf16[64,48,512]{2,1,0:T(8,128)(2,1)S(1)}, u32[]{:S(2)}, u32[]{:S(2)}) async-start(bf16[64,48,512]{2,1,0:T(8,128)(2,1)} %get-tuple-element.104), calls=%async_computation.4 | async-start | bytes 6291456 | tf_op jit(solution)/shard_map/all_to_all | solution.py:693
  160.6 0.7 slice_maximum_fusion
  161.3 0.0 collective-permute-start
  161.3 0.0 copy-done.2
  161.3 0.9 copy.20
  162.2 0.0 copy-done.1
  162.2 0.8 copy.21
  163.0 0.0 copy-done.4
  163.0 0.9 copy.18
  163.9 0.0 copy-done.3
  163.9 0.9 copy.19
  164.7 0.0 collective-permute-done
  164.7 0.6 slice.11
  166.0 0.0 copy-done.6
  166.0 6.9 %unpack_rows.2 = (bf16[512,1024]{1,0:T(8,128)(2,1)}, bf16[512,1024]{1,0:T(8,128)(2,1)}, bf16[512,1024]{1,0:T(8,128)(2,1)}, bf16[512,1024]{1,0:T(8,128)(2,1)}, f32[8,4,128]{2,1,0:T(4,128)}) custom-call(s32[1]{0:T(128)} %bitcast.5.me_ref, s32[512,4]{1,0:T(8,128)} %bitcast.24, s32[512,4]{1,0:T(8,128)} %bitcast.25, f32[8,4,128]{2,1,0:T(4,128)S(1)} %copy-done.6, ...), custom_call_target="tpu_custom_call" | custom-call | flops 3221225472 | bytes 6291456 | tf_op jit(solution)/shard_map/unpack_rows/pallas_call | solution.py:663
  172.9 26.4 %all-to-all-done.4.shared_ref.packed_ref = bf16[64,48,512]{2,1,0:T(8,128)(2,1)S(1)} async-done(((bf16[64,48,512]{2,1,0:T(8,128)(2,1)}), bf16[64,48,512]{2,1,0:T(8,128)(2,1)S(1)}, u32[]{:S(2)}, u32[]{:S(2)}) %all-to-all-start.4) | async-done | bytes 3145760 | tf_op jit(solution)/shard_map/all_to_all | solution.py:693
  199.3 6.3 %unpack_rows.3 = (bf16[512,1024]{1,0:T(8,128)(2,1)}, bf16[512,1024]{1,0:T(8,128)(2,1)}, bf16[512,1024]{1,0:T(8,128)(2,1)}, bf16[512,1024]{1,0:T(8,128)(2,1)}, f32[8,4,128]{2,1,0:T(4,128)}) custom-call(s32[1]{0:T(128)} %bitcast.5.me_ref, s32[512,4]{1,0:T(8,128)} %bitcast.22, ...), custom_call_target="tpu_custom_call", output_to_operand_aliasing={{0}: (6, {}), {1}: (7, {}), {2}: (8, {}), {3}: (9, {}), {4}... | custom-call | flops 3221225472 | bytes 6291456 | tf_op jit(solution)/shard_map/unpack_rows/pallas_call | solution.py:663
  (6 shorter events, 0.0 us)
Async XLA Ops:
  8.9 11.8 %copy-start.5 = (s32[8,512,1]{1,2,0:T(1,128)S(1)}, s32[8,512,1]{1,2,0:T(1,128)}, u32[]{:S(2)}) copy-start(s32[8,512,1]{1,2,0:T(1,128)} %param.13) | copy-start | bytes 49156
  8.9 11.8 %copy-start.7 = (s32[256]{0:T(256)S(1)}, s32[256]{0:T(256)}, u32[]{:S(2)}) copy-start(s32[256]{0:T(256)} %param.14) | copy-start | bytes 3076
  9.0 52.1 %all-to-all-start.2 = ((bf16[64,48,512]{2,1,0:T(8,128)(2,1)}), bf16[64,48,512]{2,1,0:T(8,128)(2,1)}, u32[]{:S(2)}, u32[]{:S(2)}) async-start(bf16[64,48,512]{2,1,0:T(8,128)(2,1)} %get-tuple-element.98), calls=%async_computation.2 | async-start | bytes 6291456 | tf_op jit(solution)/shard_map/all_to_all | solution.py:693
  61.1 47.8 %all-to-all-start.3 = ((bf16[64,48,512]{2,1,0:T(8,128)(2,1)}), bf16[64,48,512]{2,1,0:T(8,128)(2,1)}, u32[]{:S(2)}, u32[]{:S(2)}) async-start(bf16[64,48,512]{2,1,0:T(8,128)(2,1)} %get-tuple-element.100), calls=%async_computation.3 | async-start | bytes 6291456 | tf_op jit(solution)/shard_map/all_to_all | solution.py:693
  108.9 45.6 %all-to-all-start.5 = ((bf16[64,48,512]{2,1,0:T(8,128)(2,1)}), bf16[64,48,512]{2,1,0:T(8,128)(2,1)}, u32[]{:S(2)}, u32[]{:S(2)}) async-start(bf16[64,48,512]{2,1,0:T(8,128)(2,1)} %get-tuple-element.107), calls=%async_computation.5 | async-start | bytes 6291456 | tf_op jit(solution)/shard_map/all_to_all | solution.py:693
  154.4 6.9 %copy-start.2 = (s32[4,1,512]{2,1,0:T(1,128)S(1)}, s32[4,1,512]{2,1,0:T(1,128)}, u32[]{:S(2)}) copy-start(s32[4,1,512]{2,1,0:T(1,128)} %get-tuple-element.105) | copy-start | bytes 24580
  154.5 7.7 %copy-start.1 = (s32[4,1,512]{2,1,0:T(1,128)S(1)}, s32[4,1,512]{2,1,0:T(1,128)}, u32[]{:S(2)}) copy-start(s32[4,1,512]{2,1,0:T(1,128)} %get-tuple-element.106) | copy-start | bytes 24580
  154.5 8.6 %copy-start.4 = (s32[4,1,512]{2,1,0:T(1,128)S(1)}, s32[4,1,512]{2,1,0:T(1,128)}, u32[]{:S(2)}) copy-start(s32[4,1,512]{2,1,0:T(1,128)} %get-tuple-element.102) | copy-start | bytes 24580
  154.5 9.4 %copy-start.3 = (s32[4,1,512]{2,1,0:T(1,128)S(1)}, s32[4,1,512]{2,1,0:T(1,128)}, u32[]{:S(2)}) copy-start(s32[4,1,512]{2,1,0:T(1,128)} %get-tuple-element.103) | copy-start | bytes 24580
  154.5 11.5 %copy-start.6 = (f32[8,4,128]{2,1,0:T(4,128)S(1)}, f32[8,4,128]{2,1,0:T(4,128)}, u32[]{:S(2)}) copy-start(f32[8,4,128]{2,1,0:T(4,128)} %cent_ref.3) | copy-start | bytes 49156
  154.5 44.9 %all-to-all-start.4 = ((bf16[64,48,512]{2,1,0:T(8,128)(2,1)}), bf16[64,48,512]{2,1,0:T(8,128)(2,1)S(1)}, u32[]{:S(2)}, u32[]{:S(2)}) async-start(bf16[64,48,512]{2,1,0:T(8,128)(2,1)} %get-tuple-element.104), calls=%async_computation.4 | async-start | bytes 6291456 | tf_op jit(solution)/shard_map/all_to_all | solution.py:693
  161.3 3.4 %collective-permute-start = (f32[1,128]{1,0:T(1,128)S(1)}, f32[1,128]{1,0:T(1,128)S(1)}, u32[]{:S(2)}, u32[]{:S(2)}) collective-permute-start(f32[1,128]{1,0:T(1,128)S(1)} %slice_maximum_fusion), channel_id=1, source_target_pairs={{0,1},{1,0},{2,3},{3,2},{4,5},{5,4},{6,7},{7,6},{8,9},{9,8},{10,11... | collective-permute-start | bytes 1544 | tf_op jit(solution)/shard_map/ppermute | solution.py:705

commit v2 on v1

--- a/solution.py
+++ b/solution.py
@@ -216,8 +216,7 @@
     v_ref,
     g_ref,
     send_ref,
-    base_ref,
-    over_ref,
+    places_ref,
     header_ref,
     total_ref,
     columns_ref,
@@ -229,6 +228,9 @@
     step = pl.program_id(0)
 
     steps = columns_ref.shape[0]
+    heads = places_ref.shape[0] // 2
+    base_ref = places_ref.at[pl.ds(0, heads)]
+    over_ref = places_ref.at[pl.ds(heads, heads)]
 
     def column_copy(at_step, which):
         lanes = pl.ds((first_head + 2 * at_step) * head_size, 2 * head_size)
@@ -436,21 +438,22 @@
 
 
 def unpack_rows_kernel(
-    first_head, me_ref, base_ref, over_ref, cent_ref, shared_ref, packed_ref, *refs
+    first_head, me_ref, places_ref, cent_ref, shared_ref, packed_ref, *refs
 ):
     new_ref = refs[-1]
     out_refs = refs[-5:-1]
     owners, _, width = shared_ref.shape
     head_size = width // 4
     owned = cent_ref.shape[1]
-    tok_rows, heads = base_ref.shape
+    tok_rows, both = places_ref.shape
+    heads = both // 2
     step = pl.program_id(0)
     packed = packed_ref[...].reshape(owners * PACKED, width)
     arrived = shared_ref[...].astype(F32)
     for at in range(2):
-        here = iota((tok_rows, heads), 1) == step * 2 + at
-        base = jnp.sum(jnp.where(here, base_ref[...], 0), axis=1, keepdims=True)
-        over = jnp.sum(jnp.where(here, over_ref[...], 0), axis=1, keepdims=True)
+        lane = iota((tok_rows, both), 1) - step * 2 - at
+        base = jnp.sum(jnp.where(lane == 0, places_ref[...], 0), axis=1, keepdims=True)
+        over = jnp.sum(jnp.where(lane == heads, places_ref[...], 0), axis=1, keepdims=True)
         take = iota((tok_rows, owners * SHARED), 1) == base
         take_over = iota((tok_rows, owners * PACKED), 1) == over
         mine = arrived[:, at * SHARED : (at + 1) * SHARED, :].reshape(owners * SHARED, width)
@@ -607,8 +610,8 @@
     me_spec = pl.BlockSpec(memory_space=pltpu.SMEM)
 
     def pack(chunk):
-        row_shape = jax.ShapeDtypeStruct((heads, 1, tok_rows), jnp.int32)
-        rows_block = pl.BlockSpec((heads, 1, tok_rows), lambda s: (0, 0, 0))
+        places_shape = jax.ShapeDtypeStruct((2 * heads, 1, tok_rows), jnp.int32)
+        places_block = pl.BlockSpec((2 * heads, 1, tok_rows), lambda s: (0, 0, 0))
         return pl.pallas_call(
             functools.partial(pack_rows_kernel, chunk * heads),
             grid=(steps,),
@@ -617,8 +620,8 @@
                 pl.BlockSpec((1, cluster_count), lambda s: (0, 0)),
             ]
             + [pl.BlockSpec(memory_space=pl.ANY)] * 4,
-            out_specs=[whole_block, rows_block, rows_block],
-            out_shape=[sent_shape, row_shape, row_shape],
+            out_specs=[whole_block, places_block],
+            out_shape=[sent_shape, places_shape],
             scratch_shapes=[
                 pltpu.VMEM((seq_count, head_size), BF16),
                 pltpu.VMEM((seq_count * PACKED, width), F32),
@@ -654,9 +657,9 @@
             name="own_rows",
         )(me, received, received)
 
-    def unpack(chunk, base_rows, over_rows, returned, previous):
+    def unpack(chunk, places, returned, previous):
         column = pl.BlockSpec((tok_rows, 2 * head_size), lambda s: (0, chunk * steps + s))
-        routes_block = pl.BlockSpec((tok_rows, heads), lambda s: (0, 0))
+        places_block = pl.BlockSpec((tok_rows, 2 * heads), lambda s: (0, 0))
         centroid_block = pl.BlockSpec(
             (2, owned, head_size), lambda s: (chunk * steps + s, 0, 0)
         )
@@ -665,8 +668,7 @@
             grid=(steps,),
             in_specs=[
                 me_spec,
-                routes_block,
-                routes_block,
+                places_block,
                 centroid_block,
                 shared_block,
                 packed_block,
@@ -675,14 +677,13 @@
             out_specs=[column] * 4 + [centroid_block],
             out_shape=[pltpu.HBM((tok_rows, local_heads * head_size), BF16)] * 4
             + [pltpu.HBM(centroids.shape, F32)],
-            input_output_aliases={6 + at: at for at in range(len(previous))},
+            input_output_aliases={5 + at: at for at in range(len(previous))},
             compiler_params=params(LESS_VMEM_BYTES),
             cost_estimate=cost(2 * heads * 1536 * tok_rows * width),
             name="unpack_rows",
         )(
             me,
-            pltpu.with_memory_space_constraint(base_rows.reshape(heads, tok_rows).T, pltpu.HBM),
-            pltpu.with_memory_space_constraint(over_rows.reshape(heads, tok_rows).T, pltpu.HBM),
+            places.reshape(2 * heads, tok_rows).T,
             centroids,
             returned,
             returned,
@@ -693,12 +694,12 @@
         return lax.all_to_all(rows, "seq", split_axis=0, concat_axis=0, tiled=True)
 
     packed = [pack(chunk) for chunk in range(CHUNKS)]
-    received = [exchange(rows) for rows, _, _ in packed]
+    received = [exchange(rows) for rows, _ in packed]
     owned_now = [own(chunk, received[chunk]) for chunk in range(CHUNKS)]
     returned = [exchange(back) for back, _ in owned_now]
     outs = ()
     for chunk in range(CHUNKS):
-        outs = unpack(chunk, *packed[chunk][1:], returned[chunk], tuple(outs))
+        outs = unpack(chunk, packed[chunk][1], returned[chunk], tuple(outs))
 
     peak = functools.reduce(jnp.maximum, [seen[0:1] for _, seen in owned_now])
     swap = [(at, 1 - at) for at in range(2)]

time: 207 us -> 205 us (level)
    pallas_call x4 -> x2, local copies, waits for them, and re-layouts: 3.43 us -> 0.97 us  [pack(): pl.pallas_call(functools.partial(pack_rows_kernel, chunk * heads), grid=(...]
  transfers between devices with their start and end apart: 5 -> 5, of which waited for: 4 -> 5; matrix products, arithmetic and copies ran while one was open for 2% -> 1% of each run, Pallas kernels for 34% -> 34%
where the time goes in v2:
time: 205 us
  Pallas kernels  83.5 us (41%)
  waiting for transfers between devices  83 us (40%)
  starting transfers between devices  33.5 us (16%)
  local copies, waits for them, and re-layouts  2.52 us (1%)
    all_to_all x4, waiting for transfers between devices, exchange(): return lax.all_to_all(rows, 'seq', split_axis=0, concat_axis=0, tiled=True)  82.8 us
    pallas_call x2, Pallas kernels, own(): pl.pallas_call(functools.partial(own_rows_kernel, chunk * heads), grid=(s...  55.6 us
    all_to_all x4, starting transfers between devices, exchange(): return lax.all_to_all(rows, 'seq', split_axis=0, concat_axis=0, tiled=True)  33.5 us
    pallas_call x2, Pallas kernels, pack(): pl.pallas_call(functools.partial(pack_rows_kernel, chunk * heads), grid=(...  15.8 us
    pallas_call x2, Pallas kernels, unpack(): pl.pallas_call(functools.partial(unpack_rows_kernel, chunk * heads), grid...  12.1 us
  transfers between devices with their start and end apart: 5, of which 5 were waited for; matrix products, arithmetic and copies ran while one was open for 1% of the time, Pallas kernels for 34%

profile of v2, /device:TPU:0, one launch (start us, length us, event | category | flops | bytes accessed | tf_op | source)
XLA Modules:
  0.0 204.6 jit_solution(12103560784233829762)
XLA Ops:
  0.6 8.2 %pack_rows.2 = (bf16[64,48,512]{2,1,0:T(8,128)(2,1)}, s32[8,1,512]{2,1,0:T(1,128)}) custom-call(s32[8,1,512]{2,1,0:T(1,128)} %bitcast.18, s32[1,256]{1,0:T(1,128)} %bitcast.21, bf16[512,1024]{1,0:T(8,128)(2,1)} %q_ref.3, bf16[512,1024]{1,0:T(8,128)(2,1)} %k_ref.3, bf16[512,1024]{1,0:T(8,128)(2,1)} %v_ref.3, bf16[512,1024]{1,0:T(8,128)(2,1)} %g_ref.3), custom_call_target="tpu_custom_call" | custom-call | flops 3221225472 | bytes 6291456 | tf_op jit(solution)/shard_map/pack_rows/pallas_call | solution.py:615
  8.8 0.0 copy-start.4
  8.9 0.0 copy-start.6
  8.9 11.7 %all-to-all-start.2 = ((bf16[64,48,512]{2,1,0:T(8,128)(2,1)}), bf16[64,48,512]{2,1,0:T(8,128)(2,1)}, u32[]{:S(2)}, u32[]{:S(2)}) async-start(bf16[64,48,512]{2,1,0:T(8,128)(2,1)} %get-tuple-element.96), calls=%async_computation.2 | async-start | bytes 6291456 | tf_op jit(solution)/shard_map/all_to_all | solution.py:694
  20.6 0.0 copy-done.4
  20.6 0.0 copy-done.6
  20.6 7.6 %pack_rows.3 = (bf16[64,48,512]{2,1,0:T(8,128)(2,1)}, s32[8,1,512]{2,1,0:T(1,128)}) custom-call(s32[8,1,512]{2,1,0:T(1,128)S(1)} %bitcast.19, s32[1,256]{1,0:T(1,128)S(1)} %bitcast.22, bf16[512,1024]{1,0:T(8,128)(2,1)} %q_ref.3, bf16[512,1024]{1,0:T(8,128)(2,1)} %k_ref.3, bf16[512,1024]{1,0:T(8,128)(2,1)} %v_ref.3, bf16[512,1024]{1,0:T(8,128)(2,1)} %g_ref.3), custom_call_target="tpu_custom_call" | custom-call | flops 3221225472 | bytes 6291456 | tf_op jit(solution)/shard_map/pack_rows/pallas_call | solution.py:615
  28.2 32.8 %all-to-all-done.2.shared_ref.over_ref = bf16[64,48,512]{2,1,0:T(8,128)(2,1)} async-done(((bf16[64,48,512]{2,1,0:T(8,128)(2,1)}), bf16[64,48,512]{2,1,0:T(8,128)(2,1)}, u32[]{:S(2)}, u32[]{:S(2)}) %all-to-all-start.2) | async-done | bytes 3145760 | tf_op jit(solution)/shard_map/all_to_all | solution.py:694
  61.0 9.2 %all-to-all-start.3 = ((bf16[64,48,512]{2,1,0:T(8,128)(2,1)}), bf16[64,48,512]{2,1,0:T(8,128)(2,1)}, u32[]{:S(2)}, u32[]{:S(2)}) async-start(bf16[64,48,512]{2,1,0:T(8,128)(2,1)} %get-tuple-element.98), calls=%async_computation.3 | async-start | bytes 6291456 | tf_op jit(solution)/shard_map/all_to_all | solution.py:694
  70.2 27.8 %own_rows.2 = (bf16[64,48,512]{2,1,0:T(8,128)(2,1)}, f32[8,128]{1,0:T(8,128)}) custom-call(s32[1]{0:T(128)} %bitcast.5.me_ref, bf16[64,48,512]{2,1,0:T(8,128)(2,1)} %all-to-all-done.2.shared_ref.over_ref, bf16[64,48,512]{2,1,0:T(8,128)(2,1)} %all-to-all-done.2.shared_ref.over_ref), custom_call_target="tpu_custom_call" | custom-call | flops 4294967296 | bytes 6291456 | tf_op jit(solution)/shard_map/own_rows/pallas_call | solution.py:637
  97.9 10.9 %all-to-all-done.3.shared_ref.over_ref = bf16[64,48,512]{2,1,0:T(8,128)(2,1)} async-done(((bf16[64,48,512]{2,1,0:T(8,128)(2,1)}), bf16[64,48,512]{2,1,0:T(8,128)(2,1)}, u32[]{:S(2)}, u32[]{:S(2)}) %all-to-all-start.3) | async-done | bytes 3145760 | tf_op jit(solution)/shard_map/all_to_all | solution.py:694
  108.8 6.5 %all-to-all-start.5 = ((bf16[64,48,512]{2,1,0:T(8,128)(2,1)}), bf16[64,48,512]{2,1,0:T(8,128)(2,1)}, u32[]{:S(2)}, u32[]{:S(2)}) async-start(bf16[64,48,512]{2,1,0:T(8,128)(2,1)} %get-tuple-element.103), calls=%async_computation.5 | async-start | bytes 6291456 | tf_op jit(solution)/shard_map/all_to_all | solution.py:694
  115.3 27.9 %own_rows.3 = (bf16[64,48,512]{2,1,0:T(8,128)(2,1)}, f32[8,128]{1,0:T(8,128)}) custom-call(s32[1]{0:T(128)} %bitcast.5.me_ref, bf16[64,48,512]{2,1,0:T(8,128)(2,1)} %all-to-all-done.3.shared_ref.over_ref, bf16[64,48,512]{2,1,0:T(8,128)(2,1)} %all-to-all-done.3.shared_ref.over_ref), custom_call_target="tpu_custom_call" | custom-call | flops 4294967296 | bytes 6291456 | tf_op jit(solution)/shard_map/own_rows/pallas_call | solution.py:637
  143.1 11.2 %all-to-all-done.5.shared_ref.packed_ref = bf16[64,48,512]{2,1,0:T(8,128)(2,1)} async-done(((bf16[64,48,512]{2,1,0:T(8,128)(2,1)}), bf16[64,48,512]{2,1,0:T(8,128)(2,1)}, u32[]{:S(2)}, u32[]{:S(2)}) %all-to-all-start.5) | async-done | bytes 3145760 | tf_op jit(solution)/shard_map/all_to_all | solution.py:694
  154.4 0.0 copy-start.2
  154.4 0.0 copy-start.3
  154.4 0.0 copy-start.5
  154.4 6.1 %all-to-all-start.4 = ((bf16[64,48,512]{2,1,0:T(8,128)(2,1)}), bf16[64,48,512]{2,1,0:T(8,128)(2,1)S(1)}, u32[]{:S(2)}, u32[]{:S(2)}) async-start(bf16[64,48,512]{2,1,0:T(8,128)(2,1)} %get-tuple-element.101), calls=%async_computation.4 | async-start | bytes 6291456 | tf_op jit(solution)/shard_map/all_to_all | solution.py:694
  160.5 0.7 slice_maximum_fusion
  161.2 0.0 collective-permute-start
  161.2 0.0 copy-done.2
  161.2 0.8 copy.19
  162.0 0.0 copy-done.3
  162.0 0.1 copy.18
  162.2 0.1 collective-permute-done
  162.3 0.6 slice.11
  163.6 0.0 copy-done.5
  163.6 0.0 copy-start
  163.6 0.9 copy-done
  164.5 6.7 %unpack_rows.2 = (bf16[512,1024]{1,0:T(8,128)(2,1)}, bf16[512,1024]{1,0:T(8,128)(2,1)}, bf16[512,1024]{1,0:T(8,128)(2,1)}, bf16[512,1024]{1,0:T(8,128)(2,1)}, f32[8,4,128]{2,1,0:T(4,128)}) custom-call(s32[1]{0:T(128)} %bitcast.5.me_ref, s32[512,8]{1,0:T(8,128)S(1)} %bitcast.16, f32[8,4,128]{2,1,0:T(4,128)S(1)} %copy-done.5, ...), custom_call_target="tpu_custom_call" | custom-call | flops 3221225472 | bytes 6291456 | tf_op jit(solution)/shard_map/unpack_rows/pallas_call | solution.py:666
  171.2 28.0 %all-to-all-done.4.shared_ref.packed_ref = bf16[64,48,512]{2,1,0:T(8,128)(2,1)S(1)} async-done(((bf16[64,48,512]{2,1,0:T(8,128)(2,1)}), bf16[64,48,512]{2,1,0:T(8,128)(2,1)S(1)}, u32[]{:S(2)}, u32[]{:S(2)}) %all-to-all-start.4) | async-done | bytes 3145760 | tf_op jit(solution)/shard_map/all_to_all | solution.py:694
  199.2 5.4 %unpack_rows.3 = (bf16[512,1024]{1,0:T(8,128)(2,1)}, bf16[512,1024]{1,0:T(8,128)(2,1)}, bf16[512,1024]{1,0:T(8,128)(2,1)}, bf16[512,1024]{1,0:T(8,128)(2,1)}, f32[8,4,128]{2,1,0:T(4,128)}) custom-call(s32[1]{0:T(128)} %bitcast.5.me_ref, s32[512,8]{1,0:T(8,128)S(1)} %bitcast.15, ...), custom_call_target="tpu_custom_call", output_to_operand_aliasing={{0}: (5, {}), {1}: (6, {}), {2}: (7, {}), {3}: (8, {}), {4}... | custom-call | flops 3221225472 | bytes 6291456 | tf_op jit(solution)/shard_map/unpack_rows/pallas_call | solution.py:666
  (2 shorter events, 0.0 us)
Async XLA Ops:
  8.8 11.8 %copy-start.4 = (s32[8,512,1]{1,2,0:T(1,128)S(1)}, s32[8,512,1]{1,2,0:T(1,128)}, u32[]{:S(2)}) copy-start(s32[8,512,1]{1,2,0:T(1,128)} %param.13) | copy-start | bytes 49156
  8.9 11.8 %copy-start.6 = (s32[256]{0:T(256)S(1)}, s32[256]{0:T(256)}, u32[]{:S(2)}) copy-start(s32[256]{0:T(256)} %param.14) | copy-start | bytes 3076
  8.9 52.1 %all-to-all-start.2 = ((bf16[64,48,512]{2,1,0:T(8,128)(2,1)}), bf16[64,48,512]{2,1,0:T(8,128)(2,1)}, u32[]{:S(2)}, u32[]{:S(2)}) async-start(bf16[64,48,512]{2,1,0:T(8,128)(2,1)} %get-tuple-element.96), calls=%async_computation.2 | async-start | bytes 6291456 | tf_op jit(solution)/shard_map/all_to_all | solution.py:694
  61.0 47.8 %all-to-all-start.3 = ((bf16[64,48,512]{2,1,0:T(8,128)(2,1)}), bf16[64,48,512]{2,1,0:T(8,128)(2,1)}, u32[]{:S(2)}, u32[]{:S(2)}) async-start(bf16[64,48,512]{2,1,0:T(8,128)(2,1)} %get-tuple-element.98), calls=%async_computation.3 | async-start | bytes 6291456 | tf_op jit(solution)/shard_map/all_to_all | solution.py:694
  108.8 45.6 %all-to-all-start.5 = ((bf16[64,48,512]{2,1,0:T(8,128)(2,1)}), bf16[64,48,512]{2,1,0:T(8,128)(2,1)}, u32[]{:S(2)}, u32[]{:S(2)}) async-start(bf16[64,48,512]{2,1,0:T(8,128)(2,1)} %get-tuple-element.103), calls=%async_computation.5 | async-start | bytes 6291456 | tf_op jit(solution)/shard_map/all_to_all | solution.py:694
  154.4 6.8 %copy-start.2 = (s32[8,1,512]{2,1,0:T(1,128)S(1)}, s32[8,1,512]{2,1,0:T(1,128)}, u32[]{:S(2)}) copy-start(s32[8,1,512]{2,1,0:T(1,128)} %get-tuple-element.102) | copy-start | bytes 49156
  154.4 7.7 %copy-start.3 = (s32[8,1,512]{2,1,0:T(1,128)S(1)}, s32[8,1,512]{2,1,0:T(1,128)}, u32[]{:S(2)}) copy-start(s32[8,1,512]{2,1,0:T(1,128)} %get-tuple-element.100) | copy-start | bytes 49156
  154.4 9.2 %copy-start.5 = (f32[8,4,128]{2,1,0:T(4,128)S(1)}, f32[8,4,128]{2,1,0:T(4,128)}, u32[]{:S(2)}) copy-start(f32[8,4,128]{2,1,0:T(4,128)} %cent_ref.3) | copy-start | bytes 49156
  154.4 44.9 %all-to-all-start.4 = ((bf16[64,48,512]{2,1,0:T(8,128)(2,1)}), bf16[64,48,512]{2,1,0:T(8,128)(2,1)S(1)}, u32[]{:S(2)}, u32[]{:S(2)}) async-start(bf16[64,48,512]{2,1,0:T(8,128)(2,1)} %get-tuple-element.101), calls=%async_computation.4 | async-start | bytes 6291456 | tf_op jit(solution)/shard_map/all_to_all | solution.py:694
  161.2 1.1 collective-permute-start
  163.6 1.0 copy-start

commit v3 on v2

--- a/solution.py
+++ b/solution.py
@@ -218,14 +218,12 @@
     send_ref,
     places_ref,
     header_ref,
-    total_ref,
     columns_ref,
     arrived_ref,
 ):
     owners, send_rows, width = send_ref.shape
     tok_rows = q_ref.shape[0]
     head_size = width // 4
-    step = pl.program_id(0)
 
     steps = columns_ref.shape[0]
     heads = places_ref.shape[0] // 2
@@ -240,49 +238,34 @@
             arrived_ref.at[at_step, which],
         )
 
-    @pl.when(step == 0)
-    def _():
-        for at_step in range(steps):
-            for which in range(4):
-                column_copy(at_step, which).start()
-        find_rows(first_head, ids_ref, slot_ref, base_ref, over_ref, header_ref)
-
     for at_step in range(steps):
-
-        @pl.when(step == at_step)
-        def _():
-            for which in range(4):
-                column_copy(at_step, which).wait()
-
-    rows = [token_rows(columns_ref, step, at, head_size) for at in range(2)]
-    halves = []
-    for at in range(2):
-        place = iota((owners * SHARED, tok_rows), 0) == base_ref[step * 2 + at]
-        placed = dot(jnp.where(place, 1.0, 0.0).astype(BF16), rows[at])
-        halves.append(placed.reshape(owners, SHARED, width))
-    at_row = pl.multiple_of(step * 2 * SHARED, 2 * SHARED)
-    shared = jnp.concatenate(halves, axis=1).astype(BF16)
-    send_ref[:, pl.ds(at_row, 2 * SHARED), :] = shared
-
-    places = [
-        jnp.where(iota((owners * PACKED, tok_rows), 0) == over_ref[step * 2 + at], 1.0, 0.0).astype(BF16)
-        for at in range(2)
-    ]
-    added = dot(jnp.concatenate(places, axis=1), jnp.concatenate(rows, axis=0))
-
-    @pl.when(step == 0)
-    def _():
-        total_ref[...] = added
-
-    @pl.when(step == pl.num_programs(0) - 1)
-    def _():
-        total = total_ref[...] + added
-        last_row = iota((owners * PACKED, owners), 1) * PACKED + PACKED - 1
-        to_last = jnp.where(iota((owners * PACKED, owners), 0) == last_row, 1.0, 0.0)
-        tags = dot(to_last.astype(BF16), header_ref[...])
-        total = jnp.concatenate([total[:, :head_size] + tags, total[:, head_size:]], axis=1)
-        packed = total.astype(BF16).reshape(owners, PACKED, width)
-        send_ref[:, send_rows - PACKED :, :] = packed
+        for which in range(4):
+            column_copy(at_step, which).start()
+    find_rows(first_head, ids_ref, slot_ref, base_ref, over_ref, header_ref)
+
+    all_rows, all_places = [], []
+    for step in range(steps):
+        for which in range(4):
+            column_copy(step, which).wait()
+        rows = [token_rows(columns_ref, step, at, head_size) for at in range(2)]
+        halves = []
+        for at in range(2):
+            place = iota((owners * SHARED, tok_rows), 0) == base_ref[step * 2 + at]
+            placed = dot(jnp.where(place, 1.0, 0.0).astype(BF16), rows[at])
+            halves.append(placed.reshape(owners, SHARED, width))
+            over = iota((owners * PACKED, tok_rows), 0) == over_ref[step * 2 + at]
+            all_places.append(jnp.where(over, 1.0, 0.0).astype(BF16))
+        all_rows += rows
+        shared = jnp.concatenate(halves, axis=1).astype(BF16)
+        send_ref[:, step * 2 * SHARED : (step + 1) * 2 * SHARED, :] = shared
+
+    total = dot(jnp.concatenate(all_places, axis=1), jnp.concatenate(all_rows, axis=0))
+    last_row = iota((owners * PACKED, owners), 1) * PACKED + PACKED - 1
+    to_last = jnp.where(iota((owners * PACKED, owners), 0) == last_row, 1.0, 0.0)
+    tags = dot(to_last.astype(BF16), header_ref[...])
+    total = jnp.concatenate([total[:, :head_size] + tags, total[:, head_size:]], axis=1)
+    packed = total.astype(BF16).reshape(owners, PACKED, width)
+    send_ref[:, send_rows - PACKED :, :] = packed
 
 
 def own_rows_kernel(
@@ -614,7 +597,7 @@
         places_block = pl.BlockSpec((2 * heads, 1, tok_rows), lambda s: (0, 0, 0))
         return pl.pallas_call(
             functools.partial(pack_rows_kernel, chunk * heads),
-            grid=(steps,),
+            grid=(1,),
             in_specs=[
                 pl.BlockSpec((heads, 1, tok_rows), lambda s: (chunk, 0, 0)),
                 pl.BlockSpec((1, cluster_count), lambda s: (0, 0)),
@@ -624,7 +607,6 @@
             out_shape=[sent_shape, places_shape],
             scratch_shapes=[
                 pltpu.VMEM((seq_count, head_size), BF16),
-                pltpu.VMEM((seq_count * PACKED, width), F32),
                 pltpu.VMEM((steps, 4, tok_rows, 2 * head_size), BF16),
                 pltpu.SemaphoreType.DMA((steps, 4)),
             ],

time: 205 us -> 206 us (level)
  no operation moved by 1% of the time
where the time goes in v3:
time: 206 us; the launch traced here: 205 us
  Pallas kernels  83.7 us (41%)
  waiting for transfers between devices  82.9 us (40%)
  starting transfers between devices  33.8 us (16%)
  local copies, waits for them, and re-layouts  2.52 us (1%)
    all_to_all x4, waiting for transfers between devices, exchange(): return lax.all_to_all(rows, 'seq', split_axis=0, concat_axis=0, tiled=True)  82.8 us
    pallas_call x2, Pallas kernels, own(): pl.pallas_call(functools.partial(own_rows_kernel, chunk * heads), grid=(s...  55.6 us
    all_to_all x4, starting transfers between devices, exchange(): return lax.all_to_all(rows, 'seq', split_axis=0, concat_axis=0, tiled=True)  33.8 us
    pallas_call x2, Pallas kernels, pack(): pl.pallas_call(functools.partial(pack_rows_kernel, chunk * heads), grid=(...  16 us
    pallas_call x2, Pallas kernels, unpack(): pl.pallas_call(functools.partial(unpack_rows_kernel, chunk * heads), grid...  12.1 us
  transfers between devices with their start and end apart: 5, of which 5 were waited for; matrix products, arithmetic and copies ran while one was open for 1% of the time, Pallas kernels for 34%

profile of v3, /device:TPU:0, one launch (start us, length us, event | category | flops | bytes accessed | tf_op | source)
XLA Modules:
  0.0 205.1 jit_solution(6713079916240116514)
XLA Ops:
  0.6 8.3 %pack_rows.2 = (bf16[64,48,512]{2,1,0:T(8,128)(2,1)}, s32[8,1,512]{2,1,0:T(1,128)}) custom-call(s32[8,1,512]{2,1,0:T(1,128)} %bitcast.18, s32[1,256]{1,0:T(1,128)} %bitcast.21, bf16[512,1024]{1,0:T(8,128)(2,1)} %q_ref.3, bf16[512,1024]{1,0:T(8,128)(2,1)} %k_ref.3, bf16[512,1024]{1,0:T(8,128)(2,1)} %v_ref.3, bf16[512,1024]{1,0:T(8,128)(2,1)} %g_ref.3), custom_call_target="tpu_custom_call" | custom-call | flops 3221225472 | bytes 6291456 | tf_op jit(solution)/shard_map/pack_rows/pallas_call | solution.py:598
  8.9 0.0 copy-start.4
  9.0 0.0 copy-start.6
  9.0 11.7 %all-to-all-start.2 = ((bf16[64,48,512]{2,1,0:T(8,128)(2,1)}), bf16[64,48,512]{2,1,0:T(8,128)(2,1)}, u32[]{:S(2)}, u32[]{:S(2)}) async-start(bf16[64,48,512]{2,1,0:T(8,128)(2,1)} %get-tuple-element.96), calls=%async_computation.2 | async-start | bytes 6291456 | tf_op jit(solution)/shard_map/all_to_all | solution.py:676
  20.7 0.0 copy-done.4
  20.7 0.0 copy-done.6
  20.7 7.7 %pack_rows.3 = (bf16[64,48,512]{2,1,0:T(8,128)(2,1)}, s32[8,1,512]{2,1,0:T(1,128)}) custom-call(s32[8,1,512]{2,1,0:T(1,128)S(1)} %bitcast.19, s32[1,256]{1,0:T(1,128)S(1)} %bitcast.22, bf16[512,1024]{1,0:T(8,128)(2,1)} %q_ref.3, bf16[512,1024]{1,0:T(8,128)(2,1)} %k_ref.3, bf16[512,1024]{1,0:T(8,128)(2,1)} %v_ref.3, bf16[512,1024]{1,0:T(8,128)(2,1)} %g_ref.3), custom_call_target="tpu_custom_call" | custom-call | flops 3221225472 | bytes 6291456 | tf_op jit(solution)/shard_map/pack_rows/pallas_call | solution.py:598
  28.4 32.7 %all-to-all-done.2.shared_ref.over_ref = bf16[64,48,512]{2,1,0:T(8,128)(2,1)} async-done(((bf16[64,48,512]{2,1,0:T(8,128)(2,1)}), bf16[64,48,512]{2,1,0:T(8,128)(2,1)}, u32[]{:S(2)}, u32[]{:S(2)}) %all-to-all-start.2) | async-done | bytes 3145760 | tf_op jit(solution)/shard_map/all_to_all | solution.py:676
  61.1 9.3 %all-to-all-start.3 = ((bf16[64,48,512]{2,1,0:T(8,128)(2,1)}), bf16[64,48,512]{2,1,0:T(8,128)(2,1)}, u32[]{:S(2)}, u32[]{:S(2)}) async-start(bf16[64,48,512]{2,1,0:T(8,128)(2,1)} %get-tuple-element.98), calls=%async_computation.3 | async-start | bytes 6291456 | tf_op jit(solution)/shard_map/all_to_all | solution.py:676
  70.4 27.8 %own_rows.2 = (bf16[64,48,512]{2,1,0:T(8,128)(2,1)}, f32[8,128]{1,0:T(8,128)}) custom-call(s32[1]{0:T(128)} %bitcast.5.me_ref, bf16[64,48,512]{2,1,0:T(8,128)(2,1)} %all-to-all-done.2.shared_ref.over_ref, bf16[64,48,512]{2,1,0:T(8,128)(2,1)} %all-to-all-done.2.shared_ref.over_ref), custom_call_target="tpu_custom_call" | custom-call | flops 4294967296 | bytes 6291456 | tf_op jit(solution)/shard_map/own_rows/pallas_call | solution.py:619
  98.2 10.7 %all-to-all-done.3.shared_ref.over_ref = bf16[64,48,512]{2,1,0:T(8,128)(2,1)} async-done(((bf16[64,48,512]{2,1,0:T(8,128)(2,1)}), bf16[64,48,512]{2,1,0:T(8,128)(2,1)}, u32[]{:S(2)}, u32[]{:S(2)}) %all-to-all-start.3) | async-done | bytes 3145760 | tf_op jit(solution)/shard_map/all_to_all | solution.py:676
  108.9 6.0 %all-to-all-start.5 = ((bf16[64,48,512]{2,1,0:T(8,128)(2,1)}), bf16[64,48,512]{2,1,0:T(8,128)(2,1)}, u32[]{:S(2)}, u32[]{:S(2)}) async-start(bf16[64,48,512]{2,1,0:T(8,128)(2,1)} %get-tuple-element.103), calls=%async_computation.5 | async-start | bytes 6291456 | tf_op jit(solution)/shard_map/all_to_all | solution.py:676
  114.9 27.9 %own_rows.3 = (bf16[64,48,512]{2,1,0:T(8,128)(2,1)}, f32[8,128]{1,0:T(8,128)}) custom-call(s32[1]{0:T(128)} %bitcast.5.me_ref, bf16[64,48,512]{2,1,0:T(8,128)(2,1)} %all-to-all-done.3.shared_ref.over_ref, bf16[64,48,512]{2,1,0:T(8,128)(2,1)} %all-to-all-done.3.shared_ref.over_ref), custom_call_target="tpu_custom_call" | custom-call | flops 4294967296 | bytes 6291456 | tf_op jit(solution)/shard_map/own_rows/pallas_call | solution.py:619
  142.8 11.6 %all-to-all-done.5.shared_ref.packed_ref = bf16[64,48,512]{2,1,0:T(8,128)(2,1)} async-done(((bf16[64,48,512]{2,1,0:T(8,128)(2,1)}), bf16[64,48,512]{2,1,0:T(8,128)(2,1)}, u32[]{:S(2)}, u32[]{:S(2)}) %all-to-all-start.5) | async-done | bytes 3145760 | tf_op jit(solution)/shard_map/all_to_all | solution.py:676
  154.3 0.0 copy-start.2
  154.3 0.0 copy-start.3
  154.3 0.0 copy-start.5
  154.3 6.7 %all-to-all-start.4 = ((bf16[64,48,512]{2,1,0:T(8,128)(2,1)}), bf16[64,48,512]{2,1,0:T(8,128)(2,1)S(1)}, u32[]{:S(2)}, u32[]{:S(2)}) async-start(bf16[64,48,512]{2,1,0:T(8,128)(2,1)} %get-tuple-element.101), calls=%async_computation.4 | async-start | bytes 6291456 | tf_op jit(solution)/shard_map/all_to_all | solution.py:676
  161.1 0.7 slice_maximum_fusion
  161.8 0.0 collective-permute-start
  161.8 0.0 copy-done.2
  161.8 0.8 copy.19
  162.6 0.0 copy-done.3
  162.6 0.1 copy.18
  162.8 0.1 collective-permute-done
  162.9 0.6 slice.11
  164.2 0.0 copy-done.5
  164.2 0.0 copy-start
  164.2 0.9 copy-done
  165.1 6.7 %unpack_rows.2 = (bf16[512,1024]{1,0:T(8,128)(2,1)}, bf16[512,1024]{1,0:T(8,128)(2,1)}, bf16[512,1024]{1,0:T(8,128)(2,1)}, bf16[512,1024]{1,0:T(8,128)(2,1)}, f32[8,4,128]{2,1,0:T(4,128)}) custom-call(s32[1]{0:T(128)} %bitcast.5.me_ref, s32[512,8]{1,0:T(8,128)S(1)} %bitcast.16, f32[8,4,128]{2,1,0:T(4,128)S(1)} %copy-done.5, ...), custom_call_target="tpu_custom_call" | custom-call | flops 3221225472 | bytes 6291456 | tf_op jit(solution)/shard_map/unpack_rows/pallas_call | solution.py:648
  171.8 27.9 %all-to-all-done.4.shared_ref.packed_ref = bf16[64,48,512]{2,1,0:T(8,128)(2,1)S(1)} async-done(((bf16[64,48,512]{2,1,0:T(8,128)(2,1)}), bf16[64,48,512]{2,1,0:T(8,128)(2,1)S(1)}, u32[]{:S(2)}, u32[]{:S(2)}) %all-to-all-start.4) | async-done | bytes 3145760 | tf_op jit(solution)/shard_map/all_to_all | solution.py:676
  199.7 5.4 %unpack_rows.3 = (bf16[512,1024]{1,0:T(8,128)(2,1)}, bf16[512,1024]{1,0:T(8,128)(2,1)}, bf16[512,1024]{1,0:T(8,128)(2,1)}, bf16[512,1024]{1,0:T(8,128)(2,1)}, f32[8,4,128]{2,1,0:T(4,128)}) custom-call(s32[1]{0:T(128)} %bitcast.5.me_ref, s32[512,8]{1,0:T(8,128)S(1)} %bitcast.15, ...), custom_call_target="tpu_custom_call", output_to_operand_aliasing={{0}: (5, {}), {1}: (6, {}), {2}: (7, {}), {3}: (8, {}), {4}... | custom-call | flops 3221225472 | bytes 6291456 | tf_op jit(solution)/shard_map/unpack_rows/pallas_call | solution.py:648
  (2 shorter events, 0.0 us)
Async XLA Ops:
  8.9 11.8 %copy-start.4 = (s32[8,512,1]{1,2,0:T(1,128)S(1)}, s32[8,512,1]{1,2,0:T(1,128)}, u32[]{:S(2)}) copy-start(s32[8,512,1]{1,2,0:T(1,128)} %param.13) | copy-start | bytes 49156
  9.0 11.8 %copy-start.6 = (s32[256]{0:T(256)S(1)}, s32[256]{0:T(256)}, u32[]{:S(2)}) copy-start(s32[256]{0:T(256)} %param.14) | copy-start | bytes 3076
  9.0 52.1 %all-to-all-start.2 = ((bf16[64,48,512]{2,1,0:T(8,128)(2,1)}), bf16[64,48,512]{2,1,0:T(8,128)(2,1)}, u32[]{:S(2)}, u32[]{:S(2)}) async-start(bf16[64,48,512]{2,1,0:T(8,128)(2,1)} %get-tuple-element.96), calls=%async_computation.2 | async-start | bytes 6291456 | tf_op jit(solution)/shard_map/all_to_all | solution.py:676
  61.1 47.8 %all-to-all-start.3 = ((bf16[64,48,512]{2,1,0:T(8,128)(2,1)}), bf16[64,48,512]{2,1,0:T(8,128)(2,1)}, u32[]{:S(2)}, u32[]{:S(2)}) async-start(bf16[64,48,512]{2,1,0:T(8,128)(2,1)} %get-tuple-element.98), calls=%async_computation.3 | async-start | bytes 6291456 | tf_op jit(solution)/shard_map/all_to_all | solution.py:676
  108.9 45.4 %all-to-all-start.5 = ((bf16[64,48,512]{2,1,0:T(8,128)(2,1)}), bf16[64,48,512]{2,1,0:T(8,128)(2,1)}, u32[]{:S(2)}, u32[]{:S(2)}) async-start(bf16[64,48,512]{2,1,0:T(8,128)(2,1)} %get-tuple-element.103), calls=%async_computation.5 | async-start | bytes 6291456 | tf_op jit(solution)/shard_map/all_to_all | solution.py:676
  154.3 7.5 %copy-start.2 = (s32[8,1,512]{2,1,0:T(1,128)S(1)}, s32[8,1,512]{2,1,0:T(1,128)}, u32[]{:S(2)}) copy-start(s32[8,1,512]{2,1,0:T(1,128)} %get-tuple-element.102) | copy-start | bytes 49156
  154.3 8.3 %copy-start.3 = (s32[8,1,512]{2,1,0:T(1,128)S(1)}, s32[8,1,512]{2,1,0:T(1,128)}, u32[]{:S(2)}) copy-start(s32[8,1,512]{2,1,0:T(1,128)} %get-tuple-element.100) | copy-start | bytes 49156
  154.3 9.8 %copy-start.5 = (f32[8,4,128]{2,1,0:T(4,128)S(1)}, f32[8,4,128]{2,1,0:T(4,128)}, u32[]{:S(2)}) copy-start(f32[8,4,128]{2,1,0:T(4,128)} %cent_ref.3) | copy-start | bytes 49156
  154.3 45.4 %all-to-all-start.4 = ((bf16[64,48,512]{2,1,0:T(8,128)(2,1)}), bf16[64,48,512]{2,1,0:T(8,128)(2,1)S(1)}, u32[]{:S(2)}, u32[]{:S(2)}) async-start(bf16[64,48,512]{2,1,0:T(8,128)(2,1)} %get-tuple-element.101), calls=%async_computation.4 | async-start | bytes 6291456 | tf_op jit(solution)/shard_map/all_to_all | solution.py:676
  161.8 1.1 collective-permute-start
  164.2 1.0 copy-start
